TPU v7x, 32 devices: a whole 2x2x4 slice. The times are simulated.
32 devices in a mesh: groups: 2 (over x), slab: 8 (over z, y), chan: 2 (over core).
Axes of the slice: x: 2, y: 2, z: 4, core: 2. Of those that a mesh axis runs over, the one named last changes fastest.
Arguments:
- point_features: bfloat16 [1024, 64, 128], P(('groups', 'slab'), 'chan'), parts along dimension 0, may hold values from -6 to 6
- kernel_blocks: bfloat16 [1024, 128, 128], P(('groups', 'slab')), parts along dimension 0, may hold values from -0.5 to 0.5
- owner_slab: int32 [1024, 1], P(('groups', 'slab')), parts along dimension 0, may hold values from 0 to 7; in each aligned block of 64 rows (0 to 63, 64 to 127, ...) at most 16 rows name the same one
- tile_index: int32 [1024], P(('groups', 'slab')), parts along dimension 0, may hold values from 0 to 255
- point_count: int32 [1024], P(('groups', 'slab')), parts along dimension 0, may hold values from 32 to 128
- targets: float32 [1024, 4, 128], P(('groups', 'slab')), parts along dimension 0, may hold values from -6 to 6
- w_lift: bfloat16 [64, 64], replicated, may hold values from -0.75 to 0.75
- w_conv: bfloat16 [27, 64, 64], P(None, None, 'chan'), may hold values from -0.15625 to 0.15625
- w_out: bfloat16 [4, 64], P(None, 'chan'), may hold values from -0.75 to 0.75
Outputs:
- grad_conv: float32 [54, 64, 64], P('groups', None, 'chan'), parts along dimension 0
- grad_out: float32 [8, 64], P('groups', 'chan'), parts along dimension 0
- mean_error: float32 [2], P('groups'), parts along dimension 0
There are 2 independent parts, one for each index of `groups`. A program takes and returns all parts, laid end to end along the dimension named above; an argument that names none is the same for every part. Nothing has to cross between parts.
Inputs may be any that keep to these rules, and one draw needn't show every extreme that they name: `owner_slab`: among the 64 blocks of one device at most 16 name the same slab, a bound that some block reaches of them.
All inputs are finite; a program needn't handle non-finite values.
Results may differ from a plain program's by a relative error of at most 0.00099.
Values may be sent and summed in bfloat16 or wider, within the bound.
A program may use at most 512 MiB of HBM per device.

v0:
```python
import jax
import jax.numpy as jnp
from jax import lax
from jax.sharding import PartitionSpec as P

GX = 32
CZ = 8


HIGH = lax.Precision.HIGHEST


def extended_2(shard, sides, width):
    for axis, dim in sides:
        size, length = (lax.axis_size(axis), shard.shape[dim])
        up = [(i, (i + 1) % size) for i in range(size - 1)]
        down = [(j, i) for i, j in up]
        last = lax.slice_in_dim(shard, length - width, length, axis=dim)
        initial = lax.slice_in_dim(shard, 0, width, axis=dim)
        before = lax.ppermute(last, axis, up)
        after = lax.ppermute(initial, axis, down)
        shard = jnp.concatenate([before, shard, after], axis=dim)
    return shard


def per_device(
    point_features,
    kernel_blocks,
    owner_slab,
    tile_index,
    point_count,
    targets,
    w_lift,
    w_conv,
    w_out,
):
    owners = lax.axis_size("slab")
    blocks = point_features.shape[0]
    half_feat = point_features.shape[1]
    points = point_features.shape[2]
    width = kernel_blocks.shape[2]
    channels = w_lift.shape[1]
    half_chan = w_conv.shape[2]
    components = targets.shape[1]
    capacity = max(2, 2 * blocks // owners)
    slots = owners * capacity
    tiles = CZ * GX
    cells = tiles * width
    w_out_f = w_out.astype(jnp.float32)
    live_mask = lax.broadcasted_iota(jnp.int32, (blocks, points), 1) < point_count[:, None]
    masked = jnp.where(live_mask[:, None, :], point_features, jnp.zeros_like(point_features))
    lifted = jnp.einsum(
        "kfb,kbv->kfv", masked, kernel_blocks, preferred_element_type=jnp.float32
    ).astype(jnp.bfloat16)
    target_owner = owner_slab[:, 0]
    matches = (target_owner[:, None] == jnp.arange(owners, dtype=jnp.int32)[None, :]).astype(
        jnp.int32
    )
    earlier = jnp.cumsum(matches, axis=0) - matches
    position = target_owner * capacity + jnp.sum(earlier * matches, axis=1)
    placing = position[None, :] == jnp.arange(slots, dtype=jnp.int32)[:, None]
    place_b = placing.astype(jnp.bfloat16)
    place_f = placing.astype(jnp.float32)
    outgoing = jnp.einsum(
        "sk,kfv->sfv", place_b, lifted, preferred_element_type=jnp.float32
    ).astype(jnp.bfloat16)
    outgoing = outgoing.reshape(owners, capacity, half_feat, width)
    tile_ids = jnp.sum(jnp.where(placing, tile_index[None, :] + 1, 0), axis=1) - 1
    tile_ids = tile_ids.reshape(owners, capacity)
    arrived, arrived_ids = (
        lax.all_to_all(outgoing, "slab", split_axis=0, concat_axis=0, tiled=True),
        lax.all_to_all(tile_ids, "slab", split_axis=0, concat_axis=0, tiled=True),
    )
    selector = (
        arrived_ids.reshape(1, slots) == jnp.arange(tiles, dtype=jnp.int32)[:, None]
    ).astype(jnp.bfloat16)
    surface = jnp.einsum(
        "ts,sfv->ftv",
        selector,
        arrived.reshape(slots, half_feat, width),
        preferred_element_type=jnp.float32,
    ).astype(jnp.bfloat16)
    latent = jnp.einsum(
        "fc,ftv->ctv",
        w_lift,
        lax.all_gather(surface, "chan", axis=0, tiled=True),
        preferred_element_type=jnp.float32,
    ).astype(jnp.bfloat16)
    volume = latent.reshape(channels, CZ, GX, width)
    extended = extended_2(volume, (("slab", 1),), 1)
    kernel_oi = w_conv.reshape(3, 3, 3, channels, half_chan).transpose(4, 3, 0, 1, 2)
    hidden = lax.conv_general_dilated(
        extended[None],
        kernel_oi,
        (1, 1, 1),
        ((0, 0), (1, 1), (1, 1)),
        dimension_numbers=("NCDHW", "OIDHW", "NCDHW"),
        preferred_element_type=jnp.float32,
    )[0].reshape(half_chan, cells)
    chan_lane = lax.axis_index("chan")
    own_half = lax.dynamic_slice_in_dim(
        latent.reshape(channels, cells), chan_lane * half_chan, half_chan, 0
    )
    mixed = (
        (own_half.astype(jnp.float32) + jax.nn.silu(hidden))
        .astype(jnp.bfloat16)
        .reshape(half_chan, tiles, width)
    )
    returning = jnp.einsum(
        "ts,ctv->scv", selector, mixed, preferred_element_type=jnp.float32
    ).astype(jnp.bfloat16)
    received = lax.all_to_all(
        returning.reshape(owners, capacity, half_chan, width),
        "slab",
        split_axis=0,
        concat_axis=0,
        tiled=True,
    )
    per_block = jnp.einsum(
        "sk,scv->kcv",
        place_b,
        received.reshape(slots, half_chan, width),
        preferred_element_type=jnp.float32,
    ).astype(jnp.bfloat16)
    at_points = jnp.einsum(
        "kcv,kbv->kcb", per_block, kernel_blocks, preferred_element_type=jnp.float32
    )
    partial_pred = jnp.einsum("oc,kcb->kob", w_out_f, at_points, precision=HIGH)
    prediction = lax.psum(partial_pred, "chan")
    error = jnp.where(live_mask[:, None, :], prediction - targets, 0.0)
    doubled = (2.0 * error).astype(jnp.bfloat16)
    residue = jnp.einsum("kob,kbv->kov", doubled, kernel_blocks, preferred_element_type=jnp.float32)
    head_grads = jnp.einsum("kob,kcb->oc", doubled.astype(jnp.float32), at_points, precision=HIGH)
    block_grads = jnp.einsum("oc,kov->kcv", w_out_f, residue, precision=HIGH)
    sent_grads = jnp.einsum("sk,kcv->scv", place_f, block_grads, precision=HIGH)
    slot_grads = lax.all_to_all(
        sent_grads.reshape(owners, capacity, half_chan, width),
        "slab",
        split_axis=0,
        concat_axis=0,
        tiled=True,
    ).reshape(slots, half_chan, width)
    mixed_grads = jnp.einsum(
        "ts,scv->ctv", selector.astype(jnp.float32), slot_grads, precision=HIGH
    )
    mixed_grads = mixed_grads.reshape(half_chan, cells)
    sigmoid_h = jax.nn.sigmoid(hidden)
    hidden_grads = (mixed_grads * sigmoid_h * (1.0 + hidden * (1.0 - sigmoid_h))).astype(
        jnp.bfloat16
    )
    padded_grid = jnp.pad(extended, ((0, 0), (0, 0), (1, 1), (1, 1)))
    kernel_taps = []
    for depth in range(3):
        for across in range(3):
            for along in range(3):
                shifted = padded_grid[
                    :, depth : depth + CZ, across : across + GX, along : along + width
                ]
                kernel_taps.append(
                    jnp.einsum(
                        "ip,op->io",
                        shifted.reshape(channels, cells),
                        hidden_grads,
                        preferred_element_type=jnp.float32,
                    )
                )
    conv_terms = jnp.stack(kernel_taps, axis=0)
    squared = jnp.sum(error * error)
    point_total = jnp.sum(point_count).astype(jnp.float32)
    conv_sum, head_sum, error_sum, total_sum = lax.psum(
        (conv_terms, head_grads, squared, point_total), "slab"
    )
    factor = lax.rsqrt(components * total_sum)
    return (conv_sum * factor, head_sum * factor, (error_sum / (components * total_sum)).reshape(1))


def solution(mesh):
    placed = (
        P(("groups", "slab"), "chan", None),
        P(("groups", "slab"), None, None),
        P(("groups", "slab"), None),
        P(("groups", "slab")),
        P(("groups", "slab")),
        P(("groups", "slab"), None, None),
        P(),
        P(None, None, "chan"),
        P(None, "chan"),
    )
    return jax.shard_map(
        per_device,
        mesh=mesh,
        in_specs=placed,
        out_specs=(P("groups", None, "chan"), P("groups", "chan"), P("groups")),
        check_vma=False,
    )
```

profile of v0, /device:TPU:0, one launch (start us, length us, event | category | flops | bytes accessed | tf_op | source)
XLA Modules:
  0.0 1058.4 jit_solution(713991314936594563)
XLA Ops:
  10.5 7.3 all-to-all-start.1
  29.2 24.1 %all-to-all-done = bf16[8,16,32,128]{3,1,2,0:T(8,128)(2,1)S(1)} async-done(((bf16[8,16,32,128]{3,1,2,0:T(8,128)(2,1)}), bf16[8,16,32,128]{3,1,2,0:T(8,128)(2,1)S(1)}, u32[]{:S(2)}, u32[]{:S(2)}) %all-to-all-start) | async-done | bytes 1048608 | tf_op jit(solution)/shard_map/all_to_all | solution.py:71
  59.9 12.6 %all-gather.2.cloned.1.call-done = bf16[64,256,128]{2,1,0:T(8,128)(2,1)} async-done(((bf16[32,256,128]{2,1,0:T(8,128)(2,1)}), bf16[64,256,128]{2,1,0:T(8,128)(2,1)}) %all-gather.2.cloned.1.call-update) | async-done | bytes 4194320 | tf_op jit(solution)/shard_map/all_gather | solution.py:86
  72.5 5.8 fusion.95
  92.4 12.9 %copy.181 = bf16[64,8,32,128]{0,2,3,1:T(8,128)(2,1)} copy(bf16[64,8,32,128]{3,0,2,1:T(8,128)(2,1)} %bitcast.592) | data formatting | bytes 8388608 | tf_op jit(solution)/shard_map/reshape | solution.py:89
  114.4 10.1 fusion.449
  126.7 12.8 %copy.186 = bf16[64,10,32,1,8,17]{0,4,5,2,1,3:T(8,128)(2,1)S(1)} copy(bf16[64,10,32,1,8,17]{0,2,5,4,1,3:T(8,128)(2,1)S(1)} %bitcast.594) | data formatting | bytes 11141120 | tf_op jit(solution)/shard_map/conv_general_dilated | solution.py:92
  144.1 69.3 %broadcast_select_fusion = f32[8,32,8,17,32]{4,2,3,1,0:T(8,128)S(1)} fusion(pred[8,17]{0,1:T(8,128)(4,1)S(1)} %copy-done.44, bf16[3,3,3,64,32]{3,4,2,1,0:T(8,128)(2,1)S(1)} %bitcast.656, bf16[64,10,32,1,7,2]{0,4,5,2,1,3:T(8,128)(2,1)} %slice.122, bf16[64,10,32,1,8,17]{0,4,5,2,1,3:T(8,128)(2,1)} %copy-done.5), kind=kOutput, calls=%fused_computation.34 | convolution fusion | flops 3789946880 | bytes 10711176 | tf_op jit(solution)/shard_map/conv_general_dilated | solution.py:92
  217.4 6.2 slice_bitcast_fusion
  223.6 14.2 %copy.188 = f32[1,32,8,32,128]{4,3,2,1,0:T(8,128)} copy(f32[1,32,8,32,128]{1,3,4,2,0:T(8,128)} %slice_bitcast_fusion) | data formatting | bytes 8388608 | tf_op jit(solution)/shard_map/conv_general_dilated | solution.py:92
  237.8 4.9 reshape_squeeze.5
  247.9 35.1 %all_to_all.21 = bf16[8,16,32,128]{3,1,2,0:T(8,128)(2,1)S(1)} all-to-all(bf16[8,16,32,128]{3,1,2,0:T(8,128)(2,1)S(1)} %copy.190), channel_id=1, replica_groups=mesh['groups'=2,'slab'=8,'chan'=2] {'slab'}, dimensions={0} | all-to-all | bytes 2097152 | tf_op jit(solution)/shard_map/all_to_all | solution.py:112
  288.3 15.8 %all-reduce.5.cloned.1.call-done = f32[64,4,128]{2,1,0:T(4,128)} async-done(((f32[64,4,128]{2,1,0:T(4,128)}), f32[64,4,128]{2,1,0:T(4,128)}) %all-reduce.5.cloned.1.call-update) | async-done | bytes 131088 | tf_op jit(solution)/shard_map/psum | solution.py:129
  311.8 5.8 all-to-all-start.3
  317.6 106.5 %pad_slice_fusion = (bf16[64,8,32,128]{0,2,3,1:T(8,128)(2,1)}, bf16[64,8,32,128]{0,2,3,1:T(8,128)(2,1)}, bf16[64,8,32,128]{0,2,3,1:T(8,128)(2,1)}, bf16[64,8,32,...) fusion(bf16[64,10,32,128]{0,2,3,1:T(8,128)(2,1)} %get-tuple-ele, ...), kind=kLoop, calls=%fused_computation.10 | loop fusion | bytes 84934656 | tf_op jit(solution)/shard_map/slice | solution.py:156
  424.1 5.6 copy.197
  429.7 28.8 %pad_slice_fusion.1 = (bf16[64,8,32,128]{0,2,3,1:T(8,128)(2,1)}, bf16[64,8,32,128]{0,2,3,1:T(8,128)(2,1)}, bf16[64,8,32,128]{0,2,3,1:T(8,128)(2,1)}, bf16[64,8,32,128]{0,2,3,1:T(8,128)(2,1)}, bf16[64,8,32,128]{0,2,3,1:T(8,128)(2,1)}) fusion(bf16[64,10,32,128]{0,2,3,1:T(8,128)(2,1)} %get-tuple-element.31), kind=kLoop, calls=%fused_computation.11 | loop fusion | bytes 26214400 | tf_op jit(solution)/shard_map/slice | solution.py:156
  458.5 14.8 %copy.224 = bf16[64,8,32,128]{3,2,1,0:T(8,128)(2,1)} copy(bf16[64,8,32,128]{0,2,3,1:T(8,128)(2,1)} %get-tuple-element.25) | data formatting | bytes 8388608 | tf_op jit(solution)/shard_map/slice | solution.py:156
  473.3 14.8 %copy.222 = bf16[64,8,32,128]{3,2,1,0:T(8,128)(2,1)} copy(bf16[64,8,32,128]{0,2,3,1:T(8,128)(2,1)} %get-tuple-element.26) | data formatting | bytes 8388608 | tf_op jit(solution)/shard_map/slice | solution.py:156
  488.1 15.2 %copy.223 = bf16[64,8,32,128]{3,2,1,0:T(8,128)(2,1)} copy(bf16[64,8,32,128]{0,2,3,1:T(8,128)(2,1)} %get-tuple-element.27) | data formatting | bytes 8388608 | tf_op jit(solution)/shard_map/slice | solution.py:156
  503.3 14.8 %copy.200 = bf16[64,8,32,128]{3,2,1,0:T(8,128)(2,1)} copy(bf16[64,8,32,128]{0,2,3,1:T(8,128)(2,1)} %get-tuple-element.28) | data formatting | bytes 8388608 | tf_op jit(solution)/shard_map/slice | solution.py:156
  518.1 14.9 %copy.183 = bf16[64,8,32,128]{3,2,1,0:T(8,128)(2,1)} copy(bf16[64,8,32,128]{0,2,3,1:T(8,128)(2,1)} %get-tuple-element.29) | data formatting | bytes 8388608 | tf_op jit(solution)/shard_map/slice | solution.py:156
  532.9 14.8 %copy.225 = bf16[64,8,32,128]{3,2,1,0:T(8,128)(2,1)} copy(bf16[64,8,32,128]{0,2,3,1:T(8,128)(2,1)} %get-tuple-element.6) | data formatting | bytes 8388608 | tf_op jit(solution)/shard_map/slice | solution.py:156
  547.7 14.8 %copy.201 = bf16[64,8,32,128]{3,2,1,0:T(8,128)(2,1)} copy(bf16[64,8,32,128]{0,2,3,1:T(8,128)(2,1)} %get-tuple-element.7) | data formatting | bytes 8388608 | tf_op jit(solution)/shard_map/slice | solution.py:156
  562.6 14.8 %copy.202 = bf16[64,8,32,128]{3,2,1,0:T(8,128)(2,1)} copy(bf16[64,8,32,128]{0,2,3,1:T(8,128)(2,1)} %get-tuple-element.8) | data formatting | bytes 8388608 | tf_op jit(solution)/shard_map/slice | solution.py:156
  577.4 14.8 %copy.204 = bf16[64,8,32,128]{3,2,1,0:T(8,128)(2,1)} copy(bf16[64,8,32,128]{0,2,3,1:T(8,128)(2,1)} %get-tuple-element.9) | data formatting | bytes 8388608 | tf_op jit(solution)/shard_map/slice | solution.py:156
  592.2 15.0 %copy.205 = bf16[64,8,32,128]{3,2,1,0:T(8,128)(2,1)} copy(bf16[64,8,32,128]{0,2,3,1:T(8,128)(2,1)} %get-tuple-element.10) | data formatting | bytes 8388608 | tf_op jit(solution)/shard_map/slice | solution.py:156
  607.2 14.8 %copy.206 = bf16[64,8,32,128]{3,2,1,0:T(8,128)(2,1)} copy(bf16[64,8,32,128]{0,2,3,1:T(8,128)(2,1)} %get-tuple-element.11) | data formatting | bytes 8388608 | tf_op jit(solution)/shard_map/slice | solution.py:156
  622.0 14.8 %copy.207 = bf16[64,8,32,128]{3,2,1,0:T(8,128)(2,1)} copy(bf16[64,8,32,128]{0,2,3,1:T(8,128)(2,1)} %get-tuple-element.12) | data formatting | bytes 8388608 | tf_op jit(solution)/shard_map/slice | solution.py:156
  636.8 14.8 %copy.208 = bf16[64,8,32,128]{3,2,1,0:T(8,128)(2,1)} copy(bf16[64,8,32,128]{0,2,3,1:T(8,128)(2,1)} %get-tuple-element.13) | data formatting | bytes 8388608 | tf_op jit(solution)/shard_map/slice | solution.py:156
  651.6 14.8 %copy.209 = bf16[64,8,32,128]{3,2,1,0:T(8,128)(2,1)} copy(bf16[64,8,32,128]{0,2,3,1:T(8,128)(2,1)} %get-tuple-element.14) | data formatting | bytes 8388608 | tf_op jit(solution)/shard_map/slice | solution.py:156
  666.4 14.8 %copy.210 = bf16[64,8,32,128]{3,2,1,0:T(8,128)(2,1)} copy(bf16[64,8,32,128]{0,2,3,1:T(8,128)(2,1)} %get-tuple-element.15) | data formatting | bytes 8388608 | tf_op jit(solution)/shard_map/slice | solution.py:156
  681.3 14.8 %copy.211 = bf16[64,8,32,128]{3,2,1,0:T(8,128)(2,1)} copy(bf16[64,8,32,128]{0,2,3,1:T(8,128)(2,1)} %get-tuple-element.16) | data formatting | bytes 8388608 | tf_op jit(solution)/shard_map/slice | solution.py:156
  696.1 15.0 %copy.213 = bf16[64,8,32,128]{3,2,1,0:T(8,128)(2,1)} copy(bf16[64,8,32,128]{0,2,3,1:T(8,128)(2,1)} %get-tuple-element.17) | data formatting | bytes 8388608 | tf_op jit(solution)/shard_map/slice | solution.py:156
  711.1 14.8 %copy.214 = bf16[64,8,32,128]{3,2,1,0:T(8,128)(2,1)} copy(bf16[64,8,32,128]{0,2,3,1:T(8,128)(2,1)} %get-tuple-element.18) | data formatting | bytes 8388608 | tf_op jit(solution)/shard_map/slice | solution.py:156
  725.9 14.8 %copy.215 = bf16[64,8,32,128]{3,2,1,0:T(8,128)(2,1)} copy(bf16[64,8,32,128]{0,2,3,1:T(8,128)(2,1)} %get-tuple-element.19) | data formatting | bytes 8388608 | tf_op jit(solution)/shard_map/slice | solution.py:156
  740.7 14.8 %copy.216 = bf16[64,8,32,128]{3,2,1,0:T(8,128)(2,1)} copy(bf16[64,8,32,128]{0,2,3,1:T(8,128)(2,1)} %get-tuple-element.20) | data formatting | bytes 8388608 | tf_op jit(solution)/shard_map/slice | solution.py:156
  755.5 14.8 %copy.217 = bf16[64,8,32,128]{3,2,1,0:T(8,128)(2,1)} copy(bf16[64,8,32,128]{0,2,3,1:T(8,128)(2,1)} %get-tuple-element.21) | data formatting | bytes 8388608 | tf_op jit(solution)/shard_map/slice | solution.py:156
  770.3 14.8 %copy.218 = bf16[64,8,32,128]{3,2,1,0:T(8,128)(2,1)} copy(bf16[64,8,32,128]{0,2,3,1:T(8,128)(2,1)} %get-tuple-element.22) | data formatting | bytes 8388608 | tf_op jit(solution)/shard_map/slice | solution.py:156
  785.1 14.8 %copy.219 = bf16[64,8,32,128]{3,2,1,0:T(8,128)(2,1)} copy(bf16[64,8,32,128]{0,2,3,1:T(8,128)(2,1)} %get-tuple-element.23) | data formatting | bytes 8388608 | tf_op jit(solution)/shard_map/slice | solution.py:156
  799.9 15.2 %copy.220 = bf16[64,8,32,128]{3,2,1,0:T(8,128)(2,1)} copy(bf16[64,8,32,128]{0,2,3,1:T(8,128)(2,1)} %get-tuple-element.24) | data formatting | bytes 8388608 | tf_op jit(solution)/shard_map/slice | solution.py:156
  815.0 6.0 pad_maximum_fusion.1
  821.6 22.4 %all-reduce.1 = (f32[]{:T(128)}, f32[4,32]{1,0:T(4,128)S(1)}, f32[]{:T(128)}) all-reduce(f32[]{:T(128)S(6)} %convert_element_type.93, f32[4,32]{1,0:T(4,128)S(1)} %convolution_bitcast_fusion.2, f32[]{:T(128)} %get-tuple-element.36), channel_id=1, replica_groups=mesh['groups'=2,'slab'=8,'chan'=2] {'slab'}, use_global_device_ids=true, to_apply=%region_6.7 | all-reduce | flops 130 | bytes 1040 | tf_op jit(solution)/shard_map/psum | solution.py:170
  845.4 7.8 fusion.90
  860.9 7.2 fusion.131
  885.4 4.6 fusion.181
  961.3 4.6 fusion.351
  980.2 68.6 %all-reduce.7.cloned.1.call-done = f32[27,64,32]{1,2,0:T(8,128)} async-done(((f32[27,64,32]{1,2,0:T(8,128)}), f32[27,64,32]{1,2,0:T(8,128)}) %all-reduce.7.cloned.1.call-update) | async-done | bytes 221200 | tf_op jit(solution)/shard_map/psum | solution.py:170
  (171 shorter events, 185.3 us)
Async XLA Ops:
  7.2 11.3 %copy-start = (bf16[64,128,128]{2,1,0:T(8,128)(2,1)S(1)}, bf16[64,128,128]{2,1,0:T(8,128)(2,1)}, u32[]{:S(2)}) copy-start(bf16[64,128,128]{2,1,0:T(8,128)(2,1)} %param.10) | copy-start | bytes 6291460
  10.5 13.7 %all-to-all-start.1 = ((s32[8,1,16]{2,1,0:T(1,128)}), s32[8,1,16]{2,1,0:T(1,128)S(1)}, u32[]{:S(2)}, u32[]{:S(2)}) async-start(s32[8,1,16]{2,1,0:T(1,128)} %bitcast.4), calls=%async_computation.1 | async-start | bytes 8192 | tf_op jit(solution)/shard_map/all_to_all | solution.py:72
  24.1 29.2 %all-to-all-start = ((bf16[8,16,32,128]{3,1,2,0:T(8,128)(2,1)}), bf16[8,16,32,128]{3,1,2,0:T(8,128)(2,1)S(1)}, u32[]{:S(2)}, u32[]{:S(2)}) async-start(bf16[8,16,32,128]{3,1,2,0:T(8,128)(2,1)} %copy.171), calls=%async_computation | async-start | bytes 2097152 | tf_op jit(solution)/shard_map/all_to_all | solution.py:71
  27.9 44.6 %all-gather.2.cloned.1.call-start = ((), (), s32[]{:S(2)}) async-start(), calls=%async_computation.4 | async-start | bytes 6291456 | tf_op jit(solution)/shard_map/all_gather | solution.py:86
  29.2 218.0 %copy-start.39 = (s32[128]{0:T(128)}, s32[128]{0:T(128)S(1)}, u32[]{:S(2)}) copy-start(s32[128]{0:T(128)S(1)} %eq.47) | copy-start | bytes 1540
  53.6 18.9 %copy-start.38 = (bf16[64,64]{1,0:T(8,128)(2,1)S(1)}, bf16[64,64]{1,0:T(8,128)(2,1)}, u32[]{:S(2)}) copy-start(bf16[64,64]{1,0:T(8,128)(2,1)} %param.15) | copy-start | bytes 24580
  59.9 244.2 %all-reduce.5.cloned.1.call-start = ((), (), s32[]{:S(2)}) async-start(), calls=%async_computation.5 | async-start | bytes 262144 | tf_op jit(solution)/shard_map/psum | solution.py:129
  78.3 11.6 %copy-start.2 = (bf16[256,128,64]{1,2,0:T(8,128)(2,1)}, bf16[256,128,64]{1,2,0:T(8,128)(2,1)S(1)}, u32[]{:S(2)}) copy-start(bf16[256,128,64]{1,2,0:T(8,128)(2,1)S(1)} %fusion.95) | copy-start | bytes 12582916
  83.9 26.8 %collective-permute-start = (bf16[64,1,32,128]{3,2,1,0:T(8,128)(2,1)}, bf16[64,1,32,128]{3,2,1,0:T(8,128)(2,1)}, u32[]{:S(2)}, u32[]{:S(2)}) collective-permute-start(bf16[64,1,32,128]{3,2,1,0:T(8,128)(2,1)} %get-tuple-element.34), channel_id=1, source_target_pairs={{0,2},{2,4},{4,6},{6,8},{8,10},{10,12},{12,14},{1,3},{3,5},{5,7},{... | collective-permute-start | bytes 1572872 | tf_op jit(solution)/shard_map/ppermute | solution.py:20
  88.3 17.0 %collective-permute-start.1 = (bf16[64,1,32,128]{3,2,1,0:T(8,128)(2,1)S(1)}, bf16[64,1,32,128]{3,2,1,0:T(8,128)(2,1)}, u32[]{:S(2)}, u32[]{:S(2)}) collective-permute-start(bf16[64,1,32,128]{3,2,1,0:T(8,128)(2,1)S(1)} %get-tuple-element.35), channel_id=1, source_target_pairs={{2,0},{4,2},{6,4},{8,6},{10,8},{12,10},{14,12},{3,1},{5,3},{7,5},{... | collective-permute-start | bytes 1572872 | tf_op jit(solution)/shard_map/ppermute | solution.py:21
  126.6 17.4 %copy-start.43 = (bf16[27,64,32]{1,2,0:T(8,128)(2,1)S(1)}, bf16[27,64,32]{1,2,0:T(8,128)(2,1)}, u32[]{:S(2)}) copy-start(bf16[27,64,32]{1,2,0:T(8,128)(2,1)} %param.16) | copy-start | bytes 331780
  126.7 17.4 %copy-start.44 = (pred[8,17]{0,1:T(8,128)(4,1)S(1)}, pred[8,17]{0,1:T(8,128)(4,1)}, u32[]{:S(2)}) copy-start(pred[8,17]{0,1:T(8,128)(4,1)} %constant.40) | copy-start | bytes 412
  139.4 4.6 copy-start.5
  283.0 2.9 copy-start.41
  283.0 4.0 copy-start.42
  283.0 21.1 %copy-start.37 = (f32[64,4,128]{2,1,0:T(4,128)S(1)}, f32[64,4,128]{2,1,0:T(4,128)}, u32[]{:S(2)}) copy-start(f32[64,4,128]{2,1,0:T(4,128)} %param.14) | copy-start | bytes 393220
  311.8 533.6 %all-to-all-start.3 = ((f32[8,16,32,128]{3,2,1,0:T(8,128)}), f32[8,16,32,128]{3,2,1,0:T(8,128)}, u32[]{:S(2)}, u32[]{:S(2)}) async-start(f32[8,16,32,128]{3,2,1,0:T(8,128)} %copy.194), calls=%async_computation.3 | async-start | bytes 4194304 | tf_op jit(solution)/shard_map/all_to_all | solution.py:136
  317.6 731.2 %all-reduce.7.cloned.1.call-start = ((), (), s32[]{:S(2)}) async-start(), calls=%async_computation.6 | async-start | bytes 884736 | tf_op jit(solution)/shard_map/psum | solution.py:170
  815.0 6.0 copy-start.7
  815.0 6.0 copy-start.35
  815.0 30.4 %copy-start.40 = (s32[128]{0:T(128)S(1)}, s32[128]{0:T(128)}, u32[]{:S(2)}) copy-start(s32[128]{0:T(128)} %copy-done.39) | copy-start | bytes 1540
  860.9 7.3 copy-start.28
  860.9 7.3 copy-start.33
  868.2 4.3 copy-start.30
  872.4 4.5 copy-start.29
  876.9 4.3 copy-start.32
  881.1 4.3 copy-start.27
  885.4 4.7 copy-start.26
  890.0 4.3 copy-start.25
  894.3 4.3 copy-start.24
  898.5 4.4 copy-start.23
  902.9 4.3 copy-start.22
  907.2 4.3 copy-start.21
  911.4 4.5 copy-start.20
  915.9 4.3 copy-start.3
  921.3 5.6 copy-start.18
  926.9 4.3 copy-start.17
  931.2 4.3 copy-start.16
  935.4 4.4 copy-start.15
  939.8 4.3 copy-start.14
  944.1 4.3 copy-start.12
  948.3 4.5 copy-start.13
  952.8 4.3 copy-start.31
  957.0 4.3 copy-start.10
  961.2 4.6 copy-start.9
  965.9 4.3 copy-start.8
  970.1 4.4 copy-start.11
  974.5 76.0 %copy-start.1 = (bf16[64,128,128]{2,1,0:T(8,128)(2,1)S(1)}, bf16[64,128,128]{2,1,0:T(8,128)(2,1)}, u32[]{:S(2)}) copy-start(bf16[64,128,128]{2,1,0:T(8,128)(2,1)} %param.10) | copy-start | bytes 6291460
  (5 other events, 6.6 us)
Sparse Core Ops, SparseCore 0:
  60.0 12.4 all-gather.1
  287.1 16.9 all-reduce.4
  979.7 69.0 all-reduce.6
where the time goes:
time: 1070 us; the launch traced here: 1060 us
  local copies, waits for them, and re-layouts  595 us (56%)
  matrix products  210 us (20%)
  waiting for transfers between devices  126 us (12%)
  blocking collectives  57.5 us (5%)
  other arithmetic  28.6 us (3%)
  starting transfers between devices  22.9 us (2%)
  between operations  17.8 us (2%)
    slice x26, local copies, waits for them, and re-layouts, per_device(): padded_grid[:, depth:depth + CZ, across:across + GX, along:along + width]  492 us
    dot_general x27, matrix products, per_device(): jnp.einsum('ip,op->io', shifted.reshape(channels, cells), hidden_grads, p...  116 us
    conv_general_dilated x1, matrix products, per_device(): lax.conv_general_dilated(extended[None], kernel_oi, (1, 1, 1), ((0, 0), (...  69.3 us
    psum x1, waiting for transfers between devices, per_device(): lax.psum((conv_terms, head_grads, squared, point_total), 'slab')  68.6 us
    conv_general_dilated x5, local copies, waits for them, and re-layouts, per_device(): lax.conv_general_dilated(extended[None], kernel_oi, (1, 1, 1), ((0, 0), (...  39 us
    all_to_all x1, blocking collectives, per_device(): lax.all_to_all(returning.reshape(owners, capacity, half_chan, width), 'sl...  35.1 us
    all_to_all x1, waiting for transfers between devices, per_device(): lax.all_to_all(outgoing, 'slab', split_axis=0, concat_axis=0, tiled=True)  24.1 us
    psum x1, blocking collectives, per_device(): lax.psum((conv_terms, head_grads, squared, point_total), 'slab')  22.4 us
  transfers between devices with their start and end apart: 8, of which 6 were waited for; matrix products, arithmetic and copies ran while one was open for 50% of the time, Pallas kernels for 0%

commit v1 on v0

v1 whole, which is shorter than its diff:
```python
import jax
import jax.numpy as jnp
from jax import lax
from jax.experimental import pallas as pl
from jax.experimental.pallas import tpu as pltpu
from jax.sharding import PartitionSpec as P

GX = 32
CZ = 8


HIGH = lax.Precision.HIGHEST
VMEM_BYTES = 56 * 1024 * 1024
VMEM = pl.BlockSpec(memory_space=pltpu.VMEM)


def lift_kernel(sel_ref, own_ref, peer_ref, w_ref, out_ref, surf_ref):
    tiles, feats, width = out_ref.shape[0], w_ref.shape[1], out_ref.shape[2]
    half = feats // 2
    sel = sel_ref[...]
    for side, ref in enumerate((own_ref, peer_ref)):
        for pair in range(half // 2):
            part = jnp.dot(
                sel,
                ref[:, 2 * pair * width : 2 * (pair + 1) * width],
                preferred_element_type=jnp.float32,
            )
            for j in range(2):
                feat = side * half + 2 * pair + j
                surf_ref[pl.ds(feat, tiles, stride=feats), :] = part[:, j * width : (j + 1) * width]
    w = w_ref[...]

    def body(i, carry):
        rows = surf_ref[pl.ds(pl.multiple_of(i * 2 * feats, 2 * feats), 2 * feats), :]
        rows = rows.astype(jnp.bfloat16)
        both = jnp.concatenate([rows[:feats], rows[feats:]], axis=1)
        res = jnp.dot(w, both, preferred_element_type=jnp.float32).astype(jnp.bfloat16)
        out_ref[2 * i] = res[:, :width]
        out_ref[2 * i + 1] = res[:, width:]
        return carry

    lax.fori_loop(0, tiles // 2, body, 0, unroll=4)


def shifts(array):
    width = array.shape[1]
    lane = lax.broadcasted_iota(jnp.int32, array.shape, 1)
    right = jnp.where(lane == 0, 0.0, pltpu.roll(array, 1, 1))
    left = jnp.where(lane == width - 1, 0.0, pltpu.roll(array, width - 1, 1))
    return right, left


def patch_of(ext_ref, z, x, number):
    rows = []
    for a in range(3):
        for e in range(3):
            rows.append(
                jnp.concatenate([ext_ref[z + a, x + e + j] for j in range(number)], axis=1)
            )
    return jnp.concatenate(rows, axis=0)


def conv_kernel(lat_ref, low_ref, high_ref, w_ref, wo_ref, ext_ref, hidden_ref, mixed_ref, p_ref):
    planes, _, channels, width = ext_ref.shape
    half = hidden_ref.shape[1]
    components = p_ref.shape[1]
    zero = jnp.zeros((channels, width), ext_ref.dtype)
    for z in range(planes):
        ext_ref[z, 0] = zero
        ext_ref[z, GX + 1] = zero

    def fill(x, carry):
        ext_ref[0, x + 1] = low_ref[x]
        ext_ref[planes - 1, x + 1] = high_ref[x]
        for z in range(planes - 2):
            ext_ref[z + 1, x + 1] = lat_ref[z * GX + x]
        return carry

    lax.fori_loop(0, GX, fill, 0)
    w = w_ref[...]
    wo = wo_ref[...]

    def body(i, carry):
        z = i // (GX // 2)
        x = (i % (GX // 2)) * 2
        res = jnp.dot(w, patch_of(ext_ref, z, x, 2), preferred_element_type=jnp.float32)
        both = []
        for j in range(2):
            t = z * GX + x + j
            part = res[:, j * width : (j + 1) * width]
            right, _ = shifts(part[:half])
            _, left = shifts(part[2 * half :])
            hidden = part[half : 2 * half] + right + left
            own = ext_ref[z + 1, x + 1 + j][:half].astype(jnp.float32)
            mixed = (own + hidden * (1.0 / (1.0 + jnp.exp(-hidden)))).astype(jnp.bfloat16)
            hidden_ref[t] = hidden
            mixed_ref[t] = mixed
            both.append(mixed)
        heads = jnp.dot(wo, jnp.concatenate(both, axis=1), preferred_element_type=jnp.float32)
        for j in range(2):
            p_ref[z * GX + x + j] = heads[:components, j * width : (j + 1) * width]
        return carry

    lax.fori_loop(0, (planes - 2) * GX // 2, body, 0, unroll=2)


def grad_kernel(ext_ref, hidden_ref, mixed_ref, r_ref, wo_ref, grad_ref, head_ref):
    planes, _, _, width = ext_ref.shape
    components = r_ref.shape[1]
    number = 4
    grad_ref[...] = jnp.zeros_like(grad_ref)
    head_ref[...] = jnp.zeros_like(head_ref)

    def body(i, carry):
        z = i // (GX // number)
        x = (i % (GX // number)) * number
        columns = []
        heads = [head_ref[o] for o in range(components)]
        for j in range(number):
            t = z * GX + x + j
            hidden = hidden_ref[t]
            mixed = mixed_ref[t].astype(jnp.float32)
            res = r_ref[t]
            total = None
            for o in range(components):
                row = res[o : o + 1]
                term = wo_ref[o] * row
                total = term if total is None else total + term
                heads[o] = heads[o] + mixed * row
            s = 1.0 / (1.0 + jnp.exp(-hidden))
            grads = total * s * (1.0 + hidden * (1.0 - s))
            right, left = shifts(grads)
            columns.append(jnp.concatenate([left, grads, right], axis=0).astype(jnp.bfloat16))
        for o in range(components):
            head_ref[o] = heads[o]
        grad_ref[...] += lax.dot_general(
            patch_of(ext_ref, z, x, number),
            jnp.concatenate(columns, axis=1),
            (((1,), (1,)), ((), ())),
            preferred_element_type=jnp.float32,
        )
        return carry

    lax.fori_loop(0, (planes - 2) * GX // number, body, 0)


def call(kernel, shapes, number, flops, scratch=()):
    return pl.pallas_call(
        kernel,
        out_shape=shapes,
        in_specs=[VMEM] * number,
        out_specs=jax.tree.map(lambda _: VMEM, shapes),
        scratch_shapes=list(scratch),
        compiler_params=pltpu.CompilerParams(vmem_limit_bytes=VMEM_BYTES),
        cost_estimate=pl.CostEstimate(
            flops=flops, bytes_accessed=1 << 23, transcendentals=1 << 20
        ),
    )


def swapped_halves(array, axis, flag):
    half = array.shape[axis] // 2
    first = lax.slice_in_dim(array, 0, half, axis=axis)
    second = lax.slice_in_dim(array, half, 2 * half, axis=axis)
    return jnp.where(flag == 0, array, jnp.concatenate([second, first], axis=axis))


def exchanged(array):
    return lax.ppermute(array, "chan", [(0, 1), (1, 0)])


def to_all(array):
    return lax.all_to_all(array, "slab", split_axis=0, concat_axis=0, tiled=True)


def per_device(
    point_features,
    kernel_blocks,
    owner_slab,
    tile_index,
    point_count,
    targets,
    w_lift,
    w_conv,
    w_out,
):
    owners = lax.axis_size("slab")
    blocks = point_features.shape[0]
    half_feat = point_features.shape[1]
    points = point_features.shape[2]
    width = kernel_blocks.shape[2]
    channels = w_lift.shape[1]
    half_chan = w_conv.shape[2]
    components = targets.shape[1]
    capacity = max(2, 2 * blocks // owners)
    slots = owners * capacity
    tiles = CZ * GX
    chan_lane = lax.axis_index("chan")
    f32, bf16 = jnp.float32, jnp.bfloat16

    w_up = swapped_halves(swapped_halves(w_lift, 0, chan_lane), 1, chan_lane).T
    w_taps = swapped_halves(w_conv, 1, chan_lane).reshape(3, 3, 3, channels, half_chan)
    w_taps = w_taps.transpose(2, 4, 0, 1, 3).reshape(3 * half_chan, 9 * channels)
    w_head = jnp.pad(w_out, ((0, 16 - components), (0, 0)))
    w_spread = jnp.broadcast_to(w_out.astype(f32)[:, :, None], (components, half_chan, width))

    live_mask = lax.broadcasted_iota(jnp.int32, (blocks, points), 1) < point_count[:, None]
    masked = jnp.where(live_mask[:, None, :], point_features, jnp.zeros_like(point_features))
    lifted = jnp.einsum("kfb,kbv->kfv", masked, kernel_blocks, preferred_element_type=f32)
    lifted = lifted.astype(bf16)
    target_owner = owner_slab[:, 0]
    matches = (target_owner[:, None] == jnp.arange(owners, dtype=jnp.int32)[None, :]).astype(
        jnp.int32
    )
    earlier = jnp.cumsum(matches, axis=0) - matches
    position = target_owner * capacity + jnp.sum(earlier * matches, axis=1)
    placing = position[None, :] == jnp.arange(slots, dtype=jnp.int32)[:, None]
    place_b = placing.astype(bf16)
    place_f = placing.astype(f32)
    outgoing = jnp.einsum(
        "sk,kn->sn",
        place_b,
        lifted.reshape(blocks, half_feat * width),
        preferred_element_type=f32,
    ).astype(bf16)
    tile_ids = (jnp.sum(jnp.where(placing, tile_index[None, :] + 1, 0), axis=1) - 1).astype(bf16)
    id_lanes = jnp.broadcast_to(tile_ids[:, None], (slots, 128))
    packed = jnp.concatenate([outgoing, id_lanes], axis=1)
    arrived = to_all(packed.reshape(owners, capacity, -1)).reshape(slots, -1)
    own_slots = arrived[:, : half_feat * width]
    peer_slots = exchanged(own_slots)
    arrived_ids = arrived[:, half_feat * width].astype(f32).astype(jnp.int32)
    selecting = arrived_ids[None, :] == jnp.arange(tiles, dtype=jnp.int32)[:, None]
    select_f = selecting.astype(f32)

    latent = call(
        lift_kernel,
        jax.ShapeDtypeStruct((tiles, channels, width), bf16),
        4,
        1 << 30,
        [pltpu.VMEM((tiles * channels, width), f32)],
    )(selecting.astype(bf16), own_slots, peer_slots, w_up)

    up = [(i, i + 1) for i in range(owners - 1)]
    down = [(j, i) for i, j in up]
    before = lax.ppermute(latent[tiles - GX :], "slab", up)
    after = lax.ppermute(latent[:GX], "slab", down)
    extended, hidden, mixed, heads = call(
        conv_kernel,
        (
            jax.ShapeDtypeStruct((CZ + 2, GX + 2, channels, width), bf16),
            jax.ShapeDtypeStruct((tiles, half_chan, width), f32),
            jax.ShapeDtypeStruct((tiles, half_chan, width), bf16),
            jax.ShapeDtypeStruct((tiles, components, width), f32),
        ),
        5,
        1 << 32,
    )(latent, before, after, w_taps, w_head)

    returning = jnp.einsum(
        "ts,tn->sn", select_f, heads.reshape(tiles, components * width), precision=HIGH
    )
    received = to_all(returning.reshape(owners, capacity, -1)).reshape(slots, -1)
    per_block = jnp.einsum("sk,sn->kn", place_f, received, precision=HIGH)
    per_block = (per_block + exchanged(per_block)).reshape(blocks, components, width)
    first = lax.reduce_precision(per_block, 8, 7)
    second = lax.reduce_precision(per_block - first, 8, 7)
    third = per_block - first - second
    pieces = jnp.concatenate([first, second, third], axis=1).astype(bf16)
    terms = jnp.einsum("kqv,kbv->kqb", pieces, kernel_blocks, preferred_element_type=f32)
    terms = terms.reshape(blocks, 3, components, points)
    prediction = terms[:, 0] + (terms[:, 1] + terms[:, 2])
    error = jnp.where(live_mask[:, None, :], prediction - targets, 0.0)
    doubled = (2.0 * error).astype(bf16)
    residue = jnp.einsum("kob,kbv->kov", doubled, kernel_blocks, preferred_element_type=f32)
    sent = jnp.einsum(
        "sk,kn->sn", place_f, residue.reshape(blocks, components * width), precision=HIGH
    )
    slot_residue = to_all(sent.reshape(owners, capacity, -1)).reshape(slots, -1)
    tile_residue = jnp.einsum("ts,sn->tn", select_f, slot_residue, precision=HIGH)

    conv_terms, head_terms = call(
        grad_kernel,
        (
            jax.ShapeDtypeStruct((9 * channels, 3 * half_chan), f32),
            jax.ShapeDtypeStruct((components, half_chan, width), f32),
        ),
        5,
        1 << 32,
    )(extended, hidden, mixed, tile_residue.reshape(tiles, components, width), w_spread)

    squared = jnp.sum(error * error)
    point_total = jnp.sum(point_count).astype(f32)
    sizes = (conv_terms.size, components * half_chan)
    flat = jnp.concatenate(
        [
            conv_terms.reshape(-1),
            jnp.sum(head_terms, axis=2).reshape(-1),
            squared.reshape(1),
            point_total.reshape(1),
        ]
    )
    piece = -(-flat.shape[0] // (owners * 128)) * 128
    flat = jnp.pad(flat, (0, owners * piece - flat.shape[0])).reshape(owners, piece)
    share = jnp.sum(to_all(flat), axis=0)
    summed = to_all(jnp.broadcast_to(share[None], (owners, piece))).reshape(-1)
    conv_sum = summed[: sizes[0]].reshape(3, 3, channels, 3, half_chan)
    conv_sum = conv_sum.transpose(0, 1, 3, 2, 4).reshape(27, channels, half_chan)
    conv_sum = swapped_halves(conv_sum, 1, chan_lane)
    head_sum = summed[sizes[0] : sizes[0] + sizes[1]].reshape(components, half_chan)
    error_sum = summed[sizes[0] + sizes[1]]
    total_sum = summed[sizes[0] + sizes[1] + 1]
    factor = lax.rsqrt(components * total_sum)
    return (conv_sum * factor, head_sum * factor, (error_sum / (components * total_sum)).reshape(1))


def solution(mesh):
    placed = (
        P(("groups", "slab"), "chan", None),
        P(("groups", "slab"), None, None),
        P(("groups", "slab"), None),
        P(("groups", "slab")),
        P(("groups", "slab")),
        P(("groups", "slab"), None, None),
        P(),
        P(None, None, "chan"),
        P(None, "chan"),
    )
    return jax.shard_map(
        per_device,
        mesh=mesh,
        in_specs=placed,
        out_specs=(P("groups", None, "chan"), P("groups", "chan"), P("groups")),
        check_vma=False,
    )
```

time: 1070 us -> 248 us (0.23); the launches traced: 1060 us -> 248 us
  local copies, waits for them, and re-layouts: 595 us -> 15.2 us
  matrix products: 210 us -> 6.1 us
  Pallas kernels: 0 us -> 103 us
  waiting for transfers between devices: 126 us -> 55.7 us
  blocking collectives: 57.5 us -> 36.2 us
  other arithmetic: 28.6 us -> 10.6 us
  between operations: 17.8 us -> 4.04 us
    slice x27 -> x9, local copies, waits for them, and re-layouts: 493 us -> 3.65 us  [the longest x1 1.31 us: per_device(): after = lax.ppermute(latent[:GX], 'slab', down)]
    dot_general x38 -> x6, matrix products: 139 us -> 3.76 us  [the longest x1 1.19 us: per_device(): jnp.einsum('kqv,kbv->kqb', pieces, kernel_blocks, preferred_element_type=...]
    pallas_call x0 -> x3, Pallas kernels: none -> 103 us  [the longest x1 55.8 us: per_device(): call(conv_kernel, (jax.ShapeDtypeStruct((CZ + 2, GX + 2, channels, width)...]
    psum x2 -> x0, waiting for transfers between devices: 84.4 us -> none  [the longest x1 68.6 us: per_device(): lax.psum((conv_terms, head_grads, squared, point_total), 'slab')]
    conv_general_dilated x1 -> x0, matrix products: 69.3 us -> none  [per_device(): lax.conv_general_dilated(extended[None], kernel_oi, (1, 1, 1), ((0, 0), (...]
    conv_general_dilated x5 -> x0, local copies, waits for them, and re-layouts: 39 us -> none  [per_device(): lax.conv_general_dilated(extended[None], kernel_oi, (1, 1, 1), ((0, 0), (...]
    psum x1 -> x0, blocking collectives: 22.4 us -> none  [per_device(): lax.psum((conv_terms, head_grads, squared, point_total), 'slab')]
    ppermute x2 -> x4, waiting for transfers between devices: 2.56 us -> 21.4 us  [the longest x1 18.6 us: per_device(): before = lax.ppermute(latent[tiles - GX:], 'slab', up)]
  transfers between devices with their start and end apart: 8 -> 6, of which waited for: 6 -> 5; matrix products, arithmetic and copies ran while one was open for 50% -> 2% of each run, Pallas kernels for 0% -> 0%
where the time goes in v1:
time: 248 us
  Pallas kernels  103 us (42%)
  waiting for transfers between devices  55.7 us (22%)
  blocking collectives  36.2 us (15%)
  starting transfers between devices  16.4 us (7%)
  local copies, waits for them, and re-layouts  15.2 us (6%)
  other arithmetic  10.6 us (4%)
  matrix products  6.1 us (2%)
  between operations  4.04 us (2%)
    pallas_call x1, Pallas kernels, per_device(): call(conv_kernel, (jax.ShapeDtypeStruct((CZ + 2, GX + 2, channels, width)...  55.8 us
    all_to_all x3, blocking collectives, to_all(): lax.all_to_all(array, 'slab', split_axis=0, concat_axis=0, tiled=True)  36.2 us
    all_to_all x2, waiting for transfers between devices, to_all(): lax.all_to_all(array, 'slab', split_axis=0, concat_axis=0, tiled=True)  34.3 us
    pallas_call x1, Pallas kernels, per_device(): call(grad_kernel, (jax.ShapeDtypeStruct((9 * channels, 3 * half_chan), f3...  33.4 us
    ppermute x1, waiting for transfers between devices, per_device(): before = lax.ppermute(latent[tiles - GX:], 'slab', up)  18.6 us
    pallas_call x1, Pallas kernels, per_device(): call(lift_kernel, jax.ShapeDtypeStruct((tiles, channels, width), bf16), 4...  14.2 us
    all_to_all x2, starting transfers between devices, to_all(): lax.all_to_all(array, 'slab', split_axis=0, concat_axis=0, tiled=True)  10.9 us
  transfers between devices with their start and end apart: 6, of which 5 were waited for; matrix products, arithmetic and copies ran while one was open for 2% of the time, Pallas kernels for 0%

profile of v1, /device:TPU:0, one launch (start us, length us, event | category | flops | bytes accessed | tf_op | source)
XLA Modules:
  0.0 247.5 jit_solution(12354722251049905010)
XLA Ops:
  0.6 0.9 fusion.33
  1.6 0.8 select_reduce_fusion.1
  2.5 0.7 multiply_add_fusion.1
  3.3 0.7 iota_compare_fusion.2
  4.0 1.7 convolution_convert_fusion.1
  5.7 0.6 convolution_convert_fusion
  6.4 1.1 pad_maximum_fusion
  7.4 7.3 %all-to-all-start = ((bf16[8,16,4224]{2,1,0:T(8,128)(2,1)}), bf16[8,16,4224]{2,1,0:T(8,128)(2,1)S(1)}, u32[]{:S(2)}, u32[]{:S(2)}) async-start(bf16[8,16,4224]{2,1,0:T(8,128)(2,1)} %bitcast.52), calls=%async_computation | async-start | bytes 2162688 | tf_op jit(solution)/shard_map/all_to_all | solution.py:173
  14.8 26.4 %all-to-all-done = bf16[8,16,4224]{2,1,0:T(8,128)(2,1)S(1)} async-done(((bf16[8,16,4224]{2,1,0:T(8,128)(2,1)}), bf16[8,16,4224]{2,1,0:T(8,128)(2,1)S(1)}, u32[]{:S(2)}, u32[]{:S(2)}) %all-to-all-start) | async-done | bytes 1081376 | tf_op jit(solution)/shard_map/all_to_all | solution.py:173
  41.2 1.1 slice.81.own_ref
  42.4 0.6 fusion.34.w_ref
  43.2 0.7 fusion.18.sel_ref
  43.8 1.5 collective-permute-done.peer_ref
  45.3 14.2 %shard_map.112.lat_ref = bf16[256,64,128]{2,1,0:T(8,128)(2,1)} custom-call(bf16[256,128]{1,0:T(8,128)(2,1)} %fusion.18.sel_ref, bf16[128,4096]{1,0:T(8,128)(2,1)} %slice.81.own_ref, bf16[128,4096]{1,0:T(8,128)(2,1)} %collective-permute-done.peer_ref, bf16[64,64]{1,0:T(8,128)(2,1)} %fusion.34.w_ref), custom_call_target="tpu_custom_call" | custom-call | flops 1073741824 | bytes 8388608 | tf_op jit(solution)/shard_map/pallas_call | solution.py:236
  59.5 1.3 fusion.40
  60.8 4.1 %collective-permute-start.1 = (bf16[32,64,128]{2,1,0:T(8,128)(2,1)S(1)}, bf16[32,64,128]{2,1,0:T(8,128)(2,1)}, u32[]{:S(2)}, u32[]{:S(2)}) collective-permute-start(bf16[32,64,128]{2,1,0:T(8,128)(2,1)S(1)} %get-tuple-element.18), channel_id=1, source_target_pairs={{0,2},{2,4},{4,6},{6,8},{8,10},{10,12},{12,14},{1,3},{3,5},{5,7},{... | collective-permute-start | bytes 1572872 | tf_op jit(solution)/shard_map/ppermute | solution.py:246
  64.9 1.3 collective-permute-start.2
  66.7 0.9 reshape.166.w_ref
  67.5 0.6 pad.8.wo_ref
  68.2 18.6 %collective-permute-done.1.low_ref = bf16[32,64,128]{2,1,0:T(8,128)(2,1)} collective-permute-done((bf16[32,64,128]{2,1,0:T(8,128)(2,1)S(1)}, bf16[32,64,128]{2,1,0:T(8,128)(2,1)}, u32[]{:S(2)}, u32[]{:S(2)}) %collective-permute-start.1) | collective-permute-done | bytes 524320 | tf_op jit(solution)/shard_map/ppermute | solution.py:246
  86.8 55.8 %shard_map.113 = (bf16[10,34,64,128]{3,2,1,0:T(8,128)(2,1)}, f32[256,32,128]{2,1,0:T(8,128)}, bf16[256,32,128]{2,1,0:T(8,128)(2,1)}, f32[256,4,128]{2,1,0:T(4,128)}) custom-call(bf16[256,64,128]{2,1,0:T(8,128)(2,1)} %shard_map.112.lat_ref, bf16[32,64,128]{2,1,0:T(8,128)(2,1)} %collective-permute-done.1.low_ref, ...), custom_call_target="tpu_custom_call" | custom-call | flops 4294967296 | bytes 8388608 | tf_op jit(solution)/shard_map/pallas_call | solution.py:248
  142.6 1.3 reshape.180
  143.9 0.3 fusion.22
  144.2 13.4 %all_to_all.30 = f32[8,16,512]{2,1,0:T(8,128)S(1)} all-to-all(f32[8,16,512]{2,1,0:T(8,128)S(1)} %fusion.22), channel_id=1, replica_groups=mesh['groups'=2,'slab'=8,'chan'=2] {'slab'}, dimensions={0} | all-to-all | bytes 524288 | tf_op jit(solution)/shard_map/all_to_all | solution.py:173
  157.7 0.2 fusion.32
  158.0 1.3 collective-permute-done.3
  159.5 1.2 fusion.5
  160.9 0.6 multiply_reduce_fusion
  161.5 0.6 fusion.24
  162.2 1.0 fusion.28
  163.3 3.6 %all-to-all-start.2 = ((f32[8,16,512]{2,1,0:T(8,128)}), f32[8,16,512]{2,1,0:T(8,128)S(1)}, u32[]{:S(2)}, u32[]{:S(2)}) async-start(f32[8,16,512]{2,1,0:T(8,128)} %fusion.28), calls=%async_computation.2 | async-start | bytes 524288 | tf_op jit(solution)/shard_map/all_to_all | solution.py:173
  166.9 0.6 reduce_sum.58
  168.2 8.0 %all-to-all-done.2 = f32[8,16,512]{2,1,0:T(8,128)S(1)} async-done(((f32[8,16,512]{2,1,0:T(8,128)}), f32[8,16,512]{2,1,0:T(8,128)S(1)}, u32[]{:S(2)}, u32[]{:S(2)}) %all-to-all-start.2) | async-done | bytes 262176 | tf_op jit(solution)/shard_map/all_to_all | solution.py:173
  176.3 0.4 fusion.19
  176.7 1.1 copy.68.r_ref
  177.8 0.7 broadcast_in_dim.69.wo_ref
  178.5 33.4 %shard_map.114 = (f32[576,96]{1,0:T(8,128)}, f32[4,32,128]{2,1,0:T(8,128)}) custom-call(bf16[10,34,64,128]{3,2,1,0:T(8,128)(2,1)} %get-tuple-element.9.ext_ref, f32[256,32,128]{2,1,0:T(8,128)} %get-tuple-element.10.hidden_ref, bf16[256,32,128]{2,1,0:T(8,128)(2,1)} %get-tuple-element.11.mixed_ref, f32[256,4,128]{2,1,0:T(4,128)} %copy.68.r_ref, ...), custom_call_target="tpu_custom_call" | custom-call | flops 4294967296 | bytes 8388608 | tf_op jit(solution)/shard_map/pallas_call | solution.py:282
  211.9 1.2 reshape.173
  213.1 0.9 reduce_sum.56
  214.1 1.6 concatenate.27
  215.7 11.6 %all_to_all.31 = f32[8,1,7040]{2,1,0:T(1,128)S(1)} all-to-all(f32[8,1,7040]{2,1,0:T(1,128)S(1)} %bitcast.61), channel_id=1, replica_groups=mesh['groups'=2,'slab'=8,'chan'=2] {'slab'}, dimensions={0} | all-to-all | bytes 450560 | tf_op jit(solution)/shard_map/all_to_all | solution.py:173
  227.6 11.1 %all_to_all.32 = f32[8,1,7040]{2,1,0:T(1,128)S(1)} all-to-all(f32[8,1,7040]{2,1,0:T(1,128)S(1)} %broadcast_in_dim.70), channel_id=1, replica_groups=mesh['groups'=2,'slab'=8,'chan'=2] {'slab'}, dimensions={0} | all-to-all | bytes 450560 | tf_op jit(solution)/shard_map/all_to_all | solution.py:173
  238.7 0.6 fusion.42
  240.7 0.5 reduce.3
  241.5 1.6 reshape.178
  243.1 1.5 copy.70
  244.9 0.6 slice_multiply_fusion
  245.4 0.9 fusion.4
  (43 shorter events, 2.6 us)
Async XLA Ops:
  0.6 3.4 %copy-start = (bf16[64,128,128]{2,1,0:T(8,128)(2,1)S(1)}, bf16[64,128,128]{2,1,0:T(8,128)(2,1)}, u32[]{:S(2)}) copy-start(bf16[64,128,128]{2,1,0:T(8,128)(2,1)} %param.10) | copy-start | bytes 6291460
  6.3 8.4 %copy-start.3 = (bf16[64,64]{1,0:T(8,128)(2,1)S(1)}, bf16[64,64]{1,0:T(8,128)(2,1)}, u32[]{:S(2)}) copy-start(bf16[64,64]{1,0:T(8,128)(2,1)} %param.15) | copy-start | bytes 24580
  7.4 33.8 %all-to-all-start = ((bf16[8,16,4224]{2,1,0:T(8,128)(2,1)}), bf16[8,16,4224]{2,1,0:T(8,128)(2,1)S(1)}, u32[]{:S(2)}, u32[]{:S(2)}) async-start(bf16[8,16,4224]{2,1,0:T(8,128)(2,1)} %bitcast.52), calls=%async_computation | async-start | bytes 2162688 | tf_op jit(solution)/shard_map/all_to_all | solution.py:173
  42.3 3.0 %collective-permute-start = (bf16[128,4096]{1,0:T(8,128)(2,1)}, bf16[128,4096]{1,0:T(8,128)(2,1)}, u32[]{:S(2)}, u32[]{:S(2)}) collective-permute-start(bf16[128,4096]{1,0:T(8,128)(2,1)} %slice.81.own_ref), channel_id=1, source_target_pairs={{0,1},{1,0},{2,3},{3,2},{4,5},{5,4},{6,7},{7,6},{8,9},{9,8},{10,11... | collective-permute-start | bytes 3145736 | tf_op jit(solution)/shard_map/ppermute | solution.py:169
  59.5 6.7 %copy-start.1 = (bf16[27,64,32]{1,2,0:T(8,128)(2,1)S(1)}, bf16[27,64,32]{1,2,0:T(8,128)(2,1)}, u32[]{:S(2)}) copy-start(bf16[27,64,32]{1,2,0:T(8,128)(2,1)} %param.16) | copy-start | bytes 331780
  59.5 8.1 %copy-start.4 = (bf16[4,32]{1,0:T(4,128)(2,1)S(1)}, bf16[4,32]{1,0:T(4,128)(2,1)}, u32[]{:S(2)}) copy-start(bf16[4,32]{1,0:T(4,128)(2,1)} %param.17) | copy-start | bytes 772
  60.8 26.0 %collective-permute-start.1 = (bf16[32,64,128]{2,1,0:T(8,128)(2,1)S(1)}, bf16[32,64,128]{2,1,0:T(8,128)(2,1)}, u32[]{:S(2)}, u32[]{:S(2)}) collective-permute-start(bf16[32,64,128]{2,1,0:T(8,128)(2,1)S(1)} %get-tuple-element.18), channel_id=1, source_target_pairs={{0,2},{2,4},{4,6},{6,8},{8,10},{10,12},{12,14},{1,3},{3,5},{5,7},{... | collective-permute-start | bytes 1572872 | tf_op jit(solution)/shard_map/ppermute | solution.py:246
  64.9 21.9 %collective-permute-start.2 = (bf16[32,64,128]{2,1,0:T(8,128)(2,1)S(1)}, bf16[32,64,128]{2,1,0:T(8,128)(2,1)}, u32[]{:S(2)}, u32[]{:S(2)}) collective-permute-start(bf16[32,64,128]{2,1,0:T(8,128)(2,1)S(1)} %get-tuple-element.17), channel_id=1, source_target_pairs={{2,0},{4,2},{6,4},{8,6},{10,8},{12,10},{14,12},{3,1},{5,3},{7,5},{... | collective-permute-start | bytes 1572872 | tf_op jit(solution)/shard_map/ppermute | solution.py:247
  157.9 1.4 collective-permute-start.3
  159.4 1.4 copy-start.2
  160.9 6.0 %copy-start.5 = (s32[64]{0:T(128)S(1)}, s32[64]{0:T(128)}, u32[]{:S(2)}) copy-start(s32[64]{0:T(128)} %param.13) | copy-start | bytes 772
  163.3 12.9 %all-to-all-start.2 = ((f32[8,16,512]{2,1,0:T(8,128)}), f32[8,16,512]{2,1,0:T(8,128)S(1)}, u32[]{:S(2)}, u32[]{:S(2)}) async-start(f32[8,16,512]{2,1,0:T(8,128)} %fusion.28), calls=%async_computation.2 | async-start | bytes 524288 | tf_op jit(solution)/shard_map/all_to_all | solution.py:173

commit v2 on v1

--- a/solution.py
+++ b/solution.py
@@ -15,8 +15,13 @@
 
 
 def lift_kernel(sel_ref, own_ref, peer_ref, w_ref, out_ref, surf_ref):
-    tiles, feats, width = out_ref.shape[0], w_ref.shape[1], out_ref.shape[2]
+    width, feats = out_ref.shape[3], w_ref.shape[1]
+    tiles = sel_ref.shape[0]
     half = feats // 2
+    zero = jnp.zeros(out_ref.shape[2:], out_ref.dtype)
+    for z in range(out_ref.shape[0]):
+        out_ref[z, 0] = zero
+        out_ref[z, GX + 1] = zero
     sel = sel_ref[...]
     for side, ref in enumerate((own_ref, peer_ref)):
         for pair in range(half // 2):
@@ -35,113 +40,135 @@
         rows = rows.astype(jnp.bfloat16)
         both = jnp.concatenate([rows[:feats], rows[feats:]], axis=1)
         res = jnp.dot(w, both, preferred_element_type=jnp.float32).astype(jnp.bfloat16)
-        out_ref[2 * i] = res[:, :width]
-        out_ref[2 * i + 1] = res[:, width:]
+        z = i // (GX // 2)
+        x = (i % (GX // 2)) * 2
+        out_ref[z, x + 1] = res[:, :width]
+        out_ref[z, x + 2] = res[:, width:]
         return carry
 
     lax.fori_loop(0, tiles // 2, body, 0, unroll=4)
 
 
-def shifts(array):
+def shifted(array, by):
     width = array.shape[1]
     lane = lax.broadcasted_iota(jnp.int32, array.shape, 1)
-    right = jnp.where(lane == 0, 0.0, pltpu.roll(array, 1, 1))
-    left = jnp.where(lane == width - 1, 0.0, pltpu.roll(array, width - 1, 1))
-    return right, left
-
-
-def patch_of(ext_ref, z, x, number):
+    edge = 0 if by == 1 else width - 1
+    return jnp.where(lane == edge, 0.0, pltpu.roll(array, by % width, 1))
+
+
+def patch_of(planes, x, number):
     rows = []
-    for a in range(3):
+    for ref, z in planes:
         for e in range(3):
-            rows.append(
-                jnp.concatenate([ext_ref[z + a, x + e + j] for j in range(number)], axis=1)
-            )
+            rows.append(jnp.concatenate([ref[z, x + e + j] for j in range(number)], axis=1))
     return jnp.concatenate(rows, axis=0)
 
 
-def conv_kernel(lat_ref, low_ref, high_ref, w_ref, wo_ref, ext_ref, hidden_ref, mixed_ref, p_ref):
-    planes, _, channels, width = ext_ref.shape
-    half = hidden_ref.shape[1]
-    components = p_ref.shape[1]
-    zero = jnp.zeros((channels, width), ext_ref.dtype)
-    for z in range(planes):
-        ext_ref[z, 0] = zero
-        ext_ref[z, GX + 1] = zero
-
-    def fill(x, carry):
-        ext_ref[0, x + 1] = low_ref[x]
-        ext_ref[planes - 1, x + 1] = high_ref[x]
-        for z in range(planes - 2):
-            ext_ref[z + 1, x + 1] = lat_ref[z * GX + x]
-        return carry
-
-    lax.fori_loop(0, GX, fill, 0)
+def conv_pairs(pairs, w_ref, wo_ref, slope_ref, mixed_ref, p_ref):
+    half, width = slope_ref.shape[1:]
+    components = p_ref.shape[0] // slope_ref.shape[0]
     w = w_ref[...]
     wo = wo_ref[...]
-
-    def body(i, carry):
-        z = i // (GX // 2)
-        x = (i % (GX // 2)) * 2
-        res = jnp.dot(w, patch_of(ext_ref, z, x, 2), preferred_element_type=jnp.float32)
-        both = []
-        for j in range(2):
-            t = z * GX + x + j
-            part = res[:, j * width : (j + 1) * width]
-            right, _ = shifts(part[:half])
-            _, left = shifts(part[2 * half :])
-            hidden = part[half : 2 * half] + right + left
-            own = ext_ref[z + 1, x + 1 + j][:half].astype(jnp.float32)
-            mixed = (own + hidden * (1.0 / (1.0 + jnp.exp(-hidden)))).astype(jnp.bfloat16)
-            hidden_ref[t] = hidden
-            mixed_ref[t] = mixed
-            both.append(mixed)
-        heads = jnp.dot(wo, jnp.concatenate(both, axis=1), preferred_element_type=jnp.float32)
-        for j in range(2):
-            p_ref[z * GX + x + j] = heads[:components, j * width : (j + 1) * width]
-        return carry
-
-    lax.fori_loop(0, (planes - 2) * GX // 2, body, 0, unroll=2)
-
-
-def grad_kernel(ext_ref, hidden_ref, mixed_ref, r_ref, wo_ref, grad_ref, head_ref):
-    planes, _, _, width = ext_ref.shape
-    components = r_ref.shape[1]
-    number = 4
-    grad_ref[...] = jnp.zeros_like(grad_ref)
+    for number, planes in enumerate(pairs):
+
+        def body(i, carry, number=number, planes=planes):
+            x = i * 2
+            res = jnp.dot(w, patch_of(planes, x, 2), preferred_element_type=jnp.float32)
+            tiles = []
+            for d in range(2):
+                ref, z = planes[d + 1]
+                for j in range(2):
+                    t = (2 * number + d) * GX + x + j
+                    part = res[3 * half * d : 3 * half * (d + 1), j * width : (j + 1) * width]
+                    hidden = part[half : 2 * half] + (
+                        shifted(part[:half], 1) + shifted(part[2 * half :], -1)
+                    )
+                    s = 1.0 / (1.0 + jnp.exp(-hidden))
+                    own = ref[z, x + 1 + j][:half].astype(jnp.float32)
+                    mixed = (own + hidden * s).astype(jnp.bfloat16)
+                    slope_ref[t] = s * (1.0 + hidden * (1.0 - s))
+                    mixed_ref[t] = mixed
+                    tiles.append(mixed)
+            heads = jnp.dot(
+                wo, jnp.concatenate(tiles, axis=0), preferred_element_type=jnp.float32
+            )
+            rows = 2 * components
+            for d in range(2):
+                start = pl.multiple_of(((2 * number + d) * GX + x) * components, rows)
+                p_ref[pl.ds(start, rows), :] = heads[d * rows : (d + 1) * rows]
+            return carry
+
+        lax.fori_loop(0, GX // 2, body, 0, unroll=2)
+
+
+def inner_kernel(lat_ref, w_ref, wo_ref, slope_ref, mixed_ref, p_ref):
+    pairs = [[(lat_ref, z + k) for k in range(-1, 3)] for z in range(2, CZ - 2, 2)]
+    conv_pairs(pairs, w_ref, wo_ref, slope_ref, mixed_ref, p_ref)
+
+
+def outer_kernel(lat_ref, low_ref, high_ref, w_ref, wo_ref, slope_ref, mixed_ref, p_ref):
+    pairs = outer_pairs(lat_ref, low_ref, high_ref)
+    conv_pairs(pairs, w_ref, wo_ref, slope_ref, mixed_ref, p_ref)
+
+
+def outer_pairs(lat_ref, low_ref, high_ref):
+    first = [(low_ref, 0)] + [(lat_ref, z) for z in range(3)]
+    return [first, [(lat_ref, z) for z in range(CZ - 3, CZ)] + [(high_ref, 0)]]
+
+
+def grad_kernel(
+    lat_ref, low_ref, high_ref, inner_slope, inner_mixed, outer_slope, outer_mixed,
+    r_ref, wo_ref, grad_ref, head_ref, acc_ref,
+):
+    width = lat_ref.shape[3]
+    components, half = head_ref.shape[:2]
+    number = 8
+    acc_ref[...] = jnp.zeros_like(acc_ref)
     head_ref[...] = jnp.zeros_like(head_ref)
-
-    def body(i, carry):
-        z = i // (GX // number)
-        x = (i % (GX // number)) * number
-        columns = []
-        heads = [head_ref[o] for o in range(components)]
-        for j in range(number):
-            t = z * GX + x + j
-            hidden = hidden_ref[t]
-            mixed = mixed_ref[t].astype(jnp.float32)
-            res = r_ref[t]
-            total = None
+    ends = outer_pairs(lat_ref, low_ref, high_ref)
+    work = [(0, ends[0], outer_slope, outer_mixed, 0)]
+    for z in range(2, CZ - 2, 2):
+        planes = [(lat_ref, z + k) for k in range(-1, 3)]
+        work.append((z, planes, inner_slope, inner_mixed, z - 2))
+    work.append((CZ - 2, ends[1], outer_slope, outer_mixed, 2))
+    rest = jnp.zeros((128 - 3 * half, width), jnp.float32)
+    for z, planes, slope_ref, mixed_ref, held in work:
+
+        def body(i, carry, z=z, planes=planes, slope_ref=slope_ref, mixed_ref=mixed_ref, held=held):
+            x = i * number
+            heads = [head_ref[o] for o in range(components)]
+            sides = []
+            for d in range(2):
+                columns = []
+                place = pl.multiple_of((z + d) * GX + x, number)
+                residue = r_ref[pl.ds(place, number), :]
+                for j in range(number):
+                    t = (held + d) * GX + x + j
+                    mixed = mixed_ref[t].astype(jnp.float32)
+                    total = None
+                    for o in range(components):
+                        row = residue[j : j + 1, o * width : (o + 1) * width]
+                        term = wo_ref[o] * row
+                        total = term if total is None else total + term
+                        heads[o] = heads[o] + mixed * row
+                    grads = total * slope_ref[t]
+                    stack = [shifted(grads, -1), grads, shifted(grads, 1), rest]
+                    columns.append(jnp.concatenate(stack, axis=0).astype(jnp.bfloat16))
+                sides.append(jnp.concatenate(columns, axis=1))
             for o in range(components):
-                row = res[o : o + 1]
-                term = wo_ref[o] * row
-                total = term if total is None else total + term
-                heads[o] = heads[o] + mixed * row
-            s = 1.0 / (1.0 + jnp.exp(-hidden))
-            grads = total * s * (1.0 + hidden * (1.0 - s))
-            right, left = shifts(grads)
-            columns.append(jnp.concatenate([left, grads, right], axis=0).astype(jnp.bfloat16))
-        for o in range(components):
-            head_ref[o] = heads[o]
-        grad_ref[...] += lax.dot_general(
-            patch_of(ext_ref, z, x, number),
-            jnp.concatenate(columns, axis=1),
-            (((1,), (1,)), ((), ())),
-            preferred_element_type=jnp.float32,
-        )
-        return carry
-
-    lax.fori_loop(0, (planes - 2) * GX // number, body, 0)
+                head_ref[o] = heads[o]
+            acc_ref[...] += lax.dot_general(
+                patch_of(planes, x, number),
+                jnp.concatenate(sides, axis=0),
+                (((1,), (1,)), ((), ())),
+                preferred_element_type=jnp.float32,
+            )
+            return carry
+
+        lax.fori_loop(0, GX // number, body, 0)
+    rows = grad_ref.shape[0]
+    step = acc_ref.shape[0] - rows
+    grad_ref[...] = acc_ref[:rows, :128] + acc_ref[step:, 128:]
 
 
 def call(kernel, shapes, number, flops, scratch=()):
@@ -200,8 +227,10 @@
 
     w_up = swapped_halves(swapped_halves(w_lift, 0, chan_lane), 1, chan_lane).T
     w_taps = swapped_halves(w_conv, 1, chan_lane).reshape(3, 3, 3, channels, half_chan)
-    w_taps = w_taps.transpose(2, 4, 0, 1, 3).reshape(3 * half_chan, 9 * channels)
-    w_head = jnp.pad(w_out, ((0, 16 - components), (0, 0)))
+    w_taps = w_taps.transpose(2, 4, 0, 1, 3)
+    w_pair = [jnp.pad(w_taps, ((0, 0), (0, 0), (d, 1 - d), (0, 0), (0, 0))) for d in range(2)]
+    w_pair = jnp.stack(w_pair).reshape(6 * half_chan, 12 * channels)
+    w_head = jnp.kron(jnp.eye(4, dtype=bf16), w_out)
     w_spread = jnp.broadcast_to(w_out.astype(f32)[:, :, None], (components, half_chan, width))
 
     live_mask = lax.broadcasted_iota(jnp.int32, (blocks, points), 1) < point_count[:, None]
@@ -235,7 +264,7 @@
 
     latent = call(
         lift_kernel,
-        jax.ShapeDtypeStruct((tiles, channels, width), bf16),
+        jax.ShapeDtypeStruct((CZ, GX + 2, channels, width), bf16),
         4,
         1 << 30,
         [pltpu.VMEM((tiles * channels, width), f32)],
@@ -243,23 +272,21 @@
 
     up = [(i, i + 1) for i in range(owners - 1)]
     down = [(j, i) for i, j in up]
-    before = lax.ppermute(latent[tiles - GX :], "slab", up)
-    after = lax.ppermute(latent[:GX], "slab", down)
-    extended, hidden, mixed, heads = call(
-        conv_kernel,
-        (
-            jax.ShapeDtypeStruct((CZ + 2, GX + 2, channels, width), bf16),
-            jax.ShapeDtypeStruct((tiles, half_chan, width), f32),
-            jax.ShapeDtypeStruct((tiles, half_chan, width), bf16),
-            jax.ShapeDtypeStruct((tiles, components, width), f32),
-        ),
-        5,
-        1 << 32,
-    )(latent, before, after, w_taps, w_head)
-
+    before = lax.ppermute(latent[CZ - 1 :], "slab", up)
+    after = lax.ppermute(latent[:1], "slab", down)
+    ends = 2 * GX
+    shapes = (
+        jax.ShapeDtypeStruct((tiles // 2, half_chan, width), f32),
+        jax.ShapeDtypeStruct((tiles // 2, half_chan, width), bf16),
+        jax.ShapeDtypeStruct((tiles // 2 * components, width), f32),
+    )
+    inner = call(inner_kernel, shapes, 3, 1 << 33)(latent, w_pair, w_head)
+    outer = call(outer_kernel, shapes, 5, 1 << 33)(latent, before, after, w_pair, w_head)
+
+    outer_select = jnp.concatenate([select_f[:ends], select_f[tiles - ends :]], axis=0)
     returning = jnp.einsum(
-        "ts,tn->sn", select_f, heads.reshape(tiles, components * width), precision=HIGH
-    )
+        "ts,tn->sn", select_f[ends : tiles - ends], inner[2].reshape(tiles // 2, -1), precision=HIGH
+    ) + jnp.einsum("ts,tn->sn", outer_select, outer[2].reshape(tiles // 2, -1), precision=HIGH)
     received = to_all(returning.reshape(owners, capacity, -1)).reshape(slots, -1)
     per_block = jnp.einsum("sk,sn->kn", place_f, received, precision=HIGH)
     per_block = (per_block + exchanged(per_block)).reshape(blocks, components, width)
@@ -282,12 +309,14 @@
     conv_terms, head_terms = call(
         grad_kernel,
         (
-            jax.ShapeDtypeStruct((9 * channels, 3 * half_chan), f32),
+            jax.ShapeDtypeStruct((9 * channels, 128), f32),
             jax.ShapeDtypeStruct((components, half_chan, width), f32),
         ),
-        5,
-        1 << 32,
-    )(extended, hidden, mixed, tile_residue.reshape(tiles, components, width), w_spread)
+        9,
+        1 << 33,
+        [pltpu.VMEM((12 * channels, 256), f32)],
+    )(latent, before, after, inner[0], inner[1], outer[0], outer[1], tile_residue, w_spread)
+    conv_terms = conv_terms[:, : 3 * half_chan]
 
     squared = jnp.sum(error * error)
     point_total = jnp.sum(point_count).astype(f32)

time: 248 us -> 202 us (0.81)
  Pallas kernels: 103 us -> 68.4 us
  waiting for transfers between devices: 55.7 us -> 36.2 us
  local copies, waits for them, and re-layouts: 15.2 us -> 20.3 us
    pallas_call x3 -> x4, Pallas kernels: 103 us -> 68.4 us  [the longest x1 18.8 us: per_device(): call(outer_kernel, shapes, 5, 1 << 33)]
    ppermute x2, waiting for transfers between devices: 18.6 us -> 2.48 us  [the longest x1 2.48 us: per_device(): before = lax.ppermute(latent[CZ - 1:], 'slab', up)]
  transfers between devices with their start and end apart: 6 -> 6, of which waited for: 5 -> 4; matrix products, arithmetic and copies ran while one was open for 2% -> 5% of each run, Pallas kernels for 0% -> 9%
where the time goes in v2:
time: 202 us
  Pallas kernels  68.4 us (34%)
  waiting for transfers between devices  36.2 us (18%)
  blocking collectives  36 us (18%)
  local copies, waits for them, and re-layouts  20.3 us (10%)
  starting transfers between devices  16.4 us (8%)
  other arithmetic  12.9 us (6%)
  matrix products  7.28 us (4%)
  between operations  4.07 us (2%)
    all_to_all x3, blocking collectives, to_all(): lax.all_to_all(array, 'slab', split_axis=0, concat_axis=0, tiled=True)  36 us
    all_to_all x2, waiting for transfers between devices, to_all(): lax.all_to_all(array, 'slab', split_axis=0, concat_axis=0, tiled=True)  32.4 us
    pallas_call x1, Pallas kernels, per_device(): call(outer_kernel, shapes, 5, 1 << 33)  18.8 us
    pallas_call x1, Pallas kernels, per_device(): inner = call(inner_kernel, shapes, 3, 1 << 33)(latent, w_pair, w_head)  18.6 us
    pallas_call x1, Pallas kernels, per_device(): call(grad_kernel, (jax.ShapeDtypeStruct((9 * channels, 128), f32), jax.Sh...  16.9 us
    pallas_call x1, Pallas kernels, per_device(): call(lift_kernel, jax.ShapeDtypeStruct((CZ, GX + 2, channels, width), bf1...  14.1 us
    all_to_all x2, starting transfers between devices, to_all(): lax.all_to_all(array, 'slab', split_axis=0, concat_axis=0, tiled=True)  10.9 us
    ppermute x1, starting transfers between devices, per_device(): before = lax.ppermute(latent[CZ - 1:], 'slab', up)  4.14 us
  transfers between devices with their start and end apart: 6, of which 4 were waited for; matrix products, arithmetic and copies ran while one was open for 5% of the time, Pallas kernels for 9%

profile of v2, /device:TPU:0, one launch (start us, length us, event | category | flops | bytes accessed | tf_op | source)
XLA Modules:
  0.0 201.5 jit_solution(6358544420773848215)
XLA Ops:
  0.6 0.9 fusion.33
  1.6 0.8 select_reduce_fusion.1
  2.5 0.7 multiply_add_fusion.1
  3.3 0.7 iota_compare_fusion.2
  4.0 1.7 convolution_convert_fusion.1
  6.4 1.1 pad_maximum_fusion
  7.4 7.3 %all-to-all-start = ((bf16[8,16,4224]{2,1,0:T(8,128)(2,1)}), bf16[8,16,4224]{2,1,0:T(8,128)(2,1)S(1)}, u32[]{:S(2)}, u32[]{:S(2)}) async-start(bf16[8,16,4224]{2,1,0:T(8,128)(2,1)} %bitcast.50), calls=%async_computation | async-start | bytes 2162688 | tf_op jit(solution)/shard_map/all_to_all | solution.py:200
  15.3 1.2 pad_bitcast_fusion.1
  16.8 24.4 %all-to-all-done = bf16[8,16,4224]{2,1,0:T(8,128)(2,1)S(1)} async-done(((bf16[8,16,4224]{2,1,0:T(8,128)(2,1)}), bf16[8,16,4224]{2,1,0:T(8,128)(2,1)S(1)}, u32[]{:S(2)}, u32[]{:S(2)}) %all-to-all-start) | async-done | bytes 1081376 | tf_op jit(solution)/shard_map/all_to_all | solution.py:200
  41.2 1.1 slice.97.own_ref
  42.6 1.5 pad_maximum_fusion.1
  44.1 2.4 %reshape.163.w_ref = bf16[192,768]{1,0:T(8,128)(2,1)} reshape(bf16[2,3,32,4,3,64]{5,4,3,2,1,0:T(4,128)(2,1)} %pad_maximum_fusion.1) | data formatting | bytes 589824 | tf_op jit(solution)/shard_map/reshape | solution.py:232
  46.5 0.7 mul.69.wo_ref
  47.2 0.6 fusion.34.w_ref
  47.9 0.7 iota_compare_fusion
  48.6 14.1 %shard_map.112.lat_ref = bf16[8,34,64,128]{3,2,1,0:T(8,128)(2,1)} custom-call(bf16[256,128]{1,0:T(8,128)(2,1)} %get-tuple-element.42.sel_ref, bf16[128,4096]{1,0:T(8,128)(2,1)} %slice.97.own_ref, bf16[128,4096]{1,0:T(8,128)(2,1)} %collective-permute-done.peer_ref, bf16[64,64]{1,0:T(8,128)(2,1)} %fusion.34.w_ref), custom_call_target="tpu_custom_call" | custom-call | flops 1073741824 | bytes 8388608 | tf_op jit(solution)/shard_map/pallas_call | solution.py:265
  62.7 1.3 fusion.42
  64.0 4.1 %collective-permute-start.1 = (bf16[1,34,64,128]{3,2,1,0:T(8,128)(2,1)S(1)}, bf16[1,34,64,128]{3,2,1,0:T(8,128)(2,1)}, u32[]{:S(2)}, u32[]{:S(2)}) collective-permute-start(bf16[1,34,64,128]{3,2,1,0:T(8,128)(2,1)S(1)} %get-tuple-element.22), channel_id=1, source_target_pairs={{0,2},{2,4},{4,6},{6,8},{8,10},{10,12},{12,14},{1,3},{3,5},{5,7},{... | collective-permute-start | bytes 1671176 | tf_op jit(solution)/shard_map/ppermute | solution.py:275
  68.1 1.3 collective-permute-start.2
  69.4 18.6 %shard_map.113 = (f32[128,32,128]{2,1,0:T(8,128)}, bf16[128,32,128]{2,1,0:T(8,128)(2,1)}, f32[512,128]{1,0:T(8,128)}) custom-call(bf16[8,34,64,128]{3,2,1,0:T(8,128)(2,1)} %shard_map.112.lat_ref, bf16[192,768]{1,0:T(8,128)(2,1)} %reshape.163.w_ref, bf16[16,128]{1,0:T(8,128)(2,1)} %mul.69.wo_ref), custom_call_target="tpu_custom_call" | custom-call | flops 8589934592 | bytes 8388608 | tf_op jit(solution)/shard_map/pallas_call | solution.py:283
  88.0 1.0 reshape.164
  89.0 2.5 %collective-permute-done.1.low_ref = bf16[1,34,64,128]{3,2,1,0:T(8,128)(2,1)} collective-permute-done((bf16[1,34,64,128]{3,2,1,0:T(8,128)(2,1)S(1)}, bf16[1,34,64,128]{3,2,1,0:T(8,128)(2,1)}, u32[]{:S(2)}, u32[]{:S(2)}) %collective-permute-start.1) | collective-permute-done | bytes 557088 | tf_op jit(solution)/shard_map/ppermute | solution.py:275
  91.5 18.8 %shard_map.114 = (f32[128,32,128]{2,1,0:T(8,128)}, bf16[128,32,128]{2,1,0:T(8,128)(2,1)}, f32[512,128]{1,0:T(8,128)}) custom-call(bf16[8,34,64,128]{3,2,1,0:T(8,128)(2,1)} %shard_map.112.lat_ref, bf16[1,34,64,128]{3,2,1,0:T(8,128)(2,1)} %collective-permute-done.1.low_ref, bf16[1,34,64,128]{3,2,1,0:T(8,128)(2,1)} %collective-permute-done.2.high_ref, ...), custom_call_target="tpu_custom_call" | custom-call | flops 8589934592 | bytes 8388608 | tf_op jit(solution)/shard_map/pallas_call | solution.py:284
  110.3 1.0 reshape.165
  112.1 13.4 %all_to_all.30 = f32[8,16,512]{2,1,0:T(8,128)S(1)} all-to-all(f32[8,16,512]{2,1,0:T(8,128)S(1)} %bitcast.56), channel_id=1, replica_groups=mesh['groups'=2,'slab'=8,'chan'=2] {'slab'}, dimensions={0} | all-to-all | bytes 524288 | tf_op jit(solution)/shard_map/all_to_all | solution.py:200
  125.9 1.3 collective-permute-done.3
  127.4 1.2 fusion.5
  128.7 0.6 multiply_reduce_fusion
  129.4 0.6 fusion.24
  130.1 1.0 fusion.28
  131.1 3.6 %all-to-all-start.2 = ((f32[8,16,512]{2,1,0:T(8,128)}), f32[8,16,512]{2,1,0:T(8,128)S(1)}, u32[]{:S(2)}, u32[]{:S(2)}) async-start(f32[8,16,512]{2,1,0:T(8,128)} %fusion.28), calls=%async_computation.2 | async-start | bytes 524288 | tf_op jit(solution)/shard_map/all_to_all | solution.py:200
  134.7 0.6 reduce_sum.58
  136.0 8.0 %all-to-all-done.2 = f32[8,16,512]{2,1,0:T(8,128)S(1)} async-done(((f32[8,16,512]{2,1,0:T(8,128)}), f32[8,16,512]{2,1,0:T(8,128)S(1)}, u32[]{:S(2)}, u32[]{:S(2)}) %all-to-all-start.2) | async-done | bytes 262176 | tf_op jit(solution)/shard_map/all_to_all | solution.py:200
  144.0 1.2 fusion.17.r_ref
  145.2 0.7 broadcast_in_dim.73.wo_ref
  145.9 16.9 %shard_map.115 = (f32[576,128]{1,0:T(8,128)}, f32[4,32,128]{2,1,0:T(8,128)}) custom-call(bf16[8,34,64,128]{3,2,1,0:T(8,128)(2,1)} %shard_map.112.lat_ref, bf16[1,34,64,128]{3,2,1,0:T(8,128)(2,1)} %collective-permute-done.1.low_ref, bf16[1,34,64,128]{3,2,1,0:T(8,128)(2,1)} %collective-permute-done.2.high_ref, f32[128,32,128]{2,1,0:T(8,128)} %get-tuple-element.11.inner_slope, ...), custom_call_target="tpu_custom_call" | custom-call | flops 8589934592 | bytes 8388608 | tf_op jit(solution)/shard_map/pallas_call | solution.py:309
  162.8 1.2 reshape.172
  163.9 0.9 reduce_sum.56
  165.0 1.6 concatenate.31
  166.6 11.4 %all_to_all.31 = f32[8,1,7040]{2,1,0:T(1,128)S(1)} all-to-all(f32[8,1,7040]{2,1,0:T(1,128)S(1)} %bitcast.59), channel_id=1, replica_groups=mesh['groups'=2,'slab'=8,'chan'=2] {'slab'}, dimensions={0} | all-to-all | bytes 450560 | tf_op jit(solution)/shard_map/all_to_all | solution.py:200
  178.3 11.1 %all_to_all.32 = f32[8,1,7040]{2,1,0:T(1,128)S(1)} all-to-all(f32[8,1,7040]{2,1,0:T(1,128)S(1)} %broadcast_in_dim.74), channel_id=1, replica_groups=mesh['groups'=2,'slab'=8,'chan'=2] {'slab'}, dimensions={0} | all-to-all | bytes 450560 | tf_op jit(solution)/shard_map/all_to_all | solution.py:200
  190.1 0.7 slice.110
  192.1 1.2 reduce.2
  193.4 1.2 slice.93
  194.5 2.6 %reshape.177 = f32[3,3,64,3,32]{4,3,2,1,0:T(4,128)} reshape(f32[55296]{0:T(1024)} %slice.110) | data formatting | bytes 442368 | tf_op jit(solution)/shard_map/reshape | solution.py:336
  197.1 1.5 copy.58
  198.8 0.6 slice_multiply_fusion
  199.4 0.9 fusion.4
  (56 shorter events, 4.7 us)
Async XLA Ops:
  0.6 3.4 %copy-start = (bf16[64,128,128]{2,1,0:T(8,128)(2,1)S(1)}, bf16[64,128,128]{2,1,0:T(8,128)(2,1)}, u32[]{:S(2)}) copy-start(bf16[64,128,128]{2,1,0:T(8,128)(2,1)} %param.10) | copy-start | bytes 6291460
  6.3 8.4 %copy-start.6 = (bf16[64,64]{1,0:T(8,128)(2,1)S(1)}, bf16[64,64]{1,0:T(8,128)(2,1)}, u32[]{:S(2)}) copy-start(bf16[64,64]{1,0:T(8,128)(2,1)} %param.15) | copy-start | bytes 24580
  6.4 8.5 %copy-start.1 = (bf16[27,64,32]{1,2,0:T(8,128)(2,1)S(1)}, bf16[27,64,32]{1,2,0:T(8,128)(2,1)}, u32[]{:S(2)}) copy-start(bf16[27,64,32]{1,2,0:T(8,128)(2,1)} %param.16) | copy-start | bytes 331780
  7.4 33.8 %all-to-all-start = ((bf16[8,16,4224]{2,1,0:T(8,128)(2,1)}), bf16[8,16,4224]{2,1,0:T(8,128)(2,1)S(1)}, u32[]{:S(2)}, u32[]{:S(2)}) async-start(bf16[8,16,4224]{2,1,0:T(8,128)(2,1)} %bitcast.50), calls=%async_computation | async-start | bytes 2162688 | tf_op jit(solution)/shard_map/all_to_all | solution.py:200
  14.7 1.8 copy-start.7
  41.2 1.1 copy-start.2
  41.2 1.4 copy-start.3
  42.3 6.3 %collective-permute-start = (bf16[128,4096]{1,0:T(8,128)(2,1)}, bf16[128,4096]{1,0:T(8,128)(2,1)}, u32[]{:S(2)}, u32[]{:S(2)}) collective-permute-start(bf16[128,4096]{1,0:T(8,128)(2,1)} %slice.97.own_ref), channel_id=1, source_target_pairs={{0,1},{1,0},{2,3},{3,2},{4,5},{5,4},{6,7},{7,6},{8,9},{9,8},{10,11... | collective-permute-start | bytes 3145736 | tf_op jit(solution)/shard_map/ppermute | solution.py:196
  64.0 27.5 %collective-permute-start.1 = (bf16[1,34,64,128]{3,2,1,0:T(8,128)(2,1)S(1)}, bf16[1,34,64,128]{3,2,1,0:T(8,128)(2,1)}, u32[]{:S(2)}, u32[]{:S(2)}) collective-permute-start(bf16[1,34,64,128]{3,2,1,0:T(8,128)(2,1)S(1)} %get-tuple-element.22), channel_id=1, source_target_pairs={{0,2},{2,4},{4,6},{6,8},{8,10},{10,12},{12,14},{1,3},{3,5},{5,7},{... | collective-permute-start | bytes 1671176 | tf_op jit(solution)/shard_map/ppermute | solution.py:275
  68.1 23.4 %collective-permute-start.2 = (bf16[1,34,64,128]{3,2,1,0:T(8,128)(2,1)S(1)}, bf16[1,34,64,128]{3,2,1,0:T(8,128)(2,1)}, u32[]{:S(2)}, u32[]{:S(2)}) collective-permute-start(bf16[1,34,64,128]{3,2,1,0:T(8,128)(2,1)S(1)} %get-tuple-element.21), channel_id=1, source_target_pairs={{2,0},{4,2},{6,4},{8,6},{10,8},{12,10},{14,12},{3,1},{5,3},{7,5},{... | collective-permute-start | bytes 1671176 | tf_op jit(solution)/shard_map/ppermute | solution.py:276
  91.5 20.3 %copy-start.5 = (pred[256,128]{1,0:T(32,128)(4,1)S(1)}, pred[256,128]{1,0:T(32,128)(4,1)}, u32[]{:S(2)}) copy-start(pred[256,128]{1,0:T(32,128)(4,1)} %get-tuple-element.40) | copy-start | bytes 98308
  125.8 1.4 collective-permute-start.3
  127.3 1.4 copy-start.4
  128.7 6.0 %copy-start.9 = (s32[64]{0:T(128)S(1)}, s32[64]{0:T(128)}, u32[]{:S(2)}) copy-start(s32[64]{0:T(128)} %param.13) | copy-start | bytes 772
  129.4 15.8 %copy-start.8 = (bf16[4,32]{1,0:T(4,128)(2,1)S(1)}, bf16[4,32]{1,0:T(4,128)(2,1)}, u32[]{:S(2)}) copy-start(bf16[4,32]{1,0:T(4,128)(2,1)} %param.17) | copy-start | bytes 772
  131.1 12.9 %all-to-all-start.2 = ((f32[8,16,512]{2,1,0:T(8,128)}), f32[8,16,512]{2,1,0:T(8,128)S(1)}, u32[]{:S(2)}, u32[]{:S(2)}) async-start(f32[8,16,512]{2,1,0:T(8,128)} %fusion.28), calls=%async_computation.2 | async-start | bytes 524288 | tf_op jit(solution)/shard_map/all_to_all | solution.py:200

commit v3 on v2

--- a/solution.py
+++ b/solution.py
@@ -1,3 +1,5 @@
+import functools
+
 import jax
 import jax.numpy as jnp
 from jax import lax
@@ -196,8 +198,90 @@
     return lax.ppermute(array, "chan", [(0, 1), (1, 0)])
 
 
-def to_all(array):
+MESH = pl.DeviceIdType.MESH
+
+
+def greet_all(n, me):
+    barrier = pltpu.get_barrier_semaphore()
+
+    def greet(d, carry):
+        peer = lax.rem(me + d, n)
+        pl.semaphore_signal(barrier, inc=1, device_id={"slab": peer}, device_id_type=MESH)
+        return carry
+
+    lax.fori_loop(1, n, greet, 0)
+    pl.semaphore_wait(barrier, n - 1)
+
+
+def swap_all(n, me, source, dest_ref, send_sem, recv_sem):
+    def copy(peer, place, d):
+        return pltpu.make_async_remote_copy(
+            src_ref=source(peer),
+            dst_ref=dest_ref.at[place],
+            send_sem=send_sem.at[d],
+            recv_sem=recv_sem.at[d],
+            device_id={"slab": peer},
+            device_id_type=MESH,
+        )
+
+    def start(d, carry):
+        copy(lax.rem(me + d, n), me, d).start()
+        return carry
+
+    def finish(d, carry):
+        copy(lax.rem(me + d, n), me, d).wait_send()
+        peer = lax.rem(me + n - d, n)
+        copy(peer, peer, d).wait_recv()
+        return carry
+
+    lax.fori_loop(1, n, start, 0)
+    return lambda: lax.fori_loop(1, n, finish, 0)
+
+
+def all_to_all_kernel(n, in_ref, out_ref, send_sem, recv_sem):
+    me = lax.axis_index("slab")
+    greet_all(n, me)
+    finish = swap_all(n, me, lambda peer: in_ref.at[peer], out_ref, send_sem, recv_sem)
+    out_ref[me] = in_ref[me]
+    finish()
+
+
+def all_sum_kernel(n, in_ref, out_ref, land_ref, share_ref, send_sem, recv_sem, send2, recv2):
+    me = lax.axis_index("slab")
+    greet_all(n, me)
+    swap_all(n, me, lambda peer: in_ref.at[peer], land_ref, send_sem, recv_sem)()
+    total = lax.fori_loop(
+        1, n, lambda d, total: total + land_ref[lax.rem(me + d, n)], in_ref[me]
+    )
+    share_ref[...] = total
+    finish = swap_all(n, me, lambda peer: share_ref, out_ref, send2, recv2)
+    out_ref[me] = total
+    finish()
+
+
+def exchange_call(kernel, array, ident, pairs, scratch=()):
+    n = array.shape[0]
+    return pl.pallas_call(
+        functools.partial(kernel, n),
+        out_shape=jax.ShapeDtypeStruct(array.shape, array.dtype),
+        in_specs=[VMEM],
+        out_specs=VMEM,
+        scratch_shapes=list(scratch) + [pltpu.SemaphoreType.DMA((n,))] * (2 * pairs),
+        compiler_params=pltpu.CompilerParams(
+            collective_id=ident, has_side_effects=True, vmem_limit_bytes=VMEM_BYTES
+        ),
+    )(array)
+
+
+def to_all(array, ident):
+    if array.shape[1] % 16 == 0:
+        return exchange_call(all_to_all_kernel, array, ident, 1)
     return lax.all_to_all(array, "slab", split_axis=0, concat_axis=0, tiled=True)
+
+
+def summed_over_slab(array):
+    scratch = [pltpu.VMEM(array.shape, array.dtype), pltpu.VMEM(array.shape[1:], array.dtype)]
+    return exchange_call(all_sum_kernel, array, 3, 2, scratch)
 
 
 def per_device(
@@ -255,7 +339,7 @@
     tile_ids = (jnp.sum(jnp.where(placing, tile_index[None, :] + 1, 0), axis=1) - 1).astype(bf16)
     id_lanes = jnp.broadcast_to(tile_ids[:, None], (slots, 128))
     packed = jnp.concatenate([outgoing, id_lanes], axis=1)
-    arrived = to_all(packed.reshape(owners, capacity, -1)).reshape(slots, -1)
+    arrived = to_all(packed.reshape(owners, capacity, -1), 0).reshape(slots, -1)
     own_slots = arrived[:, : half_feat * width]
     peer_slots = exchanged(own_slots)
     arrived_ids = arrived[:, half_feat * width].astype(f32).astype(jnp.int32)
@@ -287,7 +371,7 @@
     returning = jnp.einsum(
         "ts,tn->sn", select_f[ends : tiles - ends], inner[2].reshape(tiles // 2, -1), precision=HIGH
     ) + jnp.einsum("ts,tn->sn", outer_select, outer[2].reshape(tiles // 2, -1), precision=HIGH)
-    received = to_all(returning.reshape(owners, capacity, -1)).reshape(slots, -1)
+    received = to_all(returning.reshape(owners, capacity, -1), 1).reshape(slots, -1)
     per_block = jnp.einsum("sk,sn->kn", place_f, received, precision=HIGH)
     per_block = (per_block + exchanged(per_block)).reshape(blocks, components, width)
     first = lax.reduce_precision(per_block, 8, 7)
@@ -303,7 +387,7 @@
     sent = jnp.einsum(
         "sk,kn->sn", place_f, residue.reshape(blocks, components * width), precision=HIGH
     )
-    slot_residue = to_all(sent.reshape(owners, capacity, -1)).reshape(slots, -1)
+    slot_residue = to_all(sent.reshape(owners, capacity, -1), 2).reshape(slots, -1)
     tile_residue = jnp.einsum("ts,sn->tn", select_f, slot_residue, precision=HIGH)
 
     conv_terms, head_terms = call(
@@ -329,10 +413,9 @@
             point_total.reshape(1),
         ]
     )
-    piece = -(-flat.shape[0] // (owners * 128)) * 128
-    flat = jnp.pad(flat, (0, owners * piece - flat.shape[0])).reshape(owners, piece)
-    share = jnp.sum(to_all(flat), axis=0)
-    summed = to_all(jnp.broadcast_to(share[None], (owners, piece))).reshape(-1)
+    piece = -(-flat.shape[0] // (owners * 1024)) * 1024
+    flat = jnp.pad(flat, (0, owners * piece - flat.shape[0]))
+    summed = summed_over_slab(flat.reshape(owners, piece // 128, 128)).reshape(-1)
     conv_sum = summed[: sizes[0]].reshape(3, 3, channels, 3, half_chan)
     conv_sum = conv_sum.transpose(0, 1, 3, 2, 4).reshape(27, channels, half_chan)
     conv_sum = swapped_halves(conv_sum, 1, chan_lane)

time: 202 us -> 197 us (0.975)
  Pallas kernels: 68.4 us -> 140 us
  blocking collectives: 36 us -> 0 us
  waiting for transfers between devices: 36.2 us -> 2.6 us
  starting transfers between devices: 16.4 us -> 6.91 us
  matrix products: 7.28 us -> 9.89 us
    pallas_call x0 -> x4, Pallas kernels: none -> 72.1 us  [exchange_call(): pl.pallas_call(functools.partial(kernel, n), out_shape=jax.ShapeDtypeStru...]
    all_to_all x3 -> x0, blocking collectives: 36 us -> none  [to_all(): lax.all_to_all(array, 'slab', split_axis=0, concat_axis=0, tiled=True)]
    all_to_all x2 -> x0, waiting for transfers between devices: 32.4 us -> none  [to_all(): lax.all_to_all(array, 'slab', split_axis=0, concat_axis=0, tiled=True)]
    all_to_all x2 -> x0, starting transfers between devices: 10.9 us -> none  [to_all(): lax.all_to_all(array, 'slab', split_axis=0, concat_axis=0, tiled=True)]
  transfers between devices with their start and end apart: 6 -> 4, of which waited for: 4 -> 1; matrix products, arithmetic and copies ran while one was open for 5% -> 5% of each run, Pallas kernels for 9% -> 9%
where the time goes in v3:
time: 197 us; the launch traced here: 196 us
  Pallas kernels  140 us (71%)
  local copies, waits for them, and re-layouts  20 us (10%)
  other arithmetic  12.3 us (6%)
  matrix products  9.89 us (5%)
  starting transfers between devices  6.91 us (4%)
  between operations  4.09 us (2%)
  waiting for transfers between devices  2.6 us (1%)
    pallas_call x4, Pallas kernels, exchange_call(): pl.pallas_call(functools.partial(kernel, n), out_shape=jax.ShapeDtypeStru...  72.1 us
    pallas_call x1, Pallas kernels, per_device(): call(outer_kernel, shapes, 5, 1 << 33)  18.8 us
    pallas_call x1, Pallas kernels, per_device(): inner = call(inner_kernel, shapes, 3, 1 << 33)(latent, w_pair, w_head)  18.6 us
    pallas_call x1, Pallas kernels, per_device(): call(grad_kernel, (jax.ShapeDtypeStruct((9 * channels, 128), f32), jax.Sh...  16.9 us
    pallas_call x1, Pallas kernels, per_device(): call(lift_kernel, jax.ShapeDtypeStruct((CZ, GX + 2, channels, width), bf1...  14.1 us
    ppermute x1, starting transfers between devices, per_device(): before = lax.ppermute(latent[CZ - 1:], 'slab', up)  5.31 us
  transfers between devices with their start and end apart: 4, of which 1 were waited for; matrix products, arithmetic and copies ran while one was open for 5% of the time, Pallas kernels for 9%

profile of v3, /device:TPU:0, one launch (start us, length us, event | category | flops | bytes accessed | tf_op | source)
XLA Modules:
  0.0 196.3 jit_solution(2950222790416375878)
XLA Ops:
  0.6 0.9 fusion.33
  1.6 0.8 select_reduce_fusion.1
  2.5 0.7 multiply_add_fusion.1
  3.3 0.7 iota_compare_fusion.2
  4.0 1.7 convolution_convert_fusion.1
  5.7 0.6 convolution_convert_fusion
  6.3 1.1 pad_maximum_fusion
  7.4 25.8 %shard_map.112 = bf16[8,16,4224]{2,1,0:T(8,128)(2,1)} custom-call(bf16[8,16,4224]{2,1,0:T(8,128)(2,1)} %bitcast.50), custom_call_target="tpu_custom_call" | custom-call | tf_op jit(solution)/shard_map/pallas_call | solution.py:264
  33.2 1.3 slice.97.own_ref
  35.8 1.6 pad_maximum_fusion.1
  37.4 2.4 %reshape.155.w_ref = bf16[192,768]{1,0:T(8,128)(2,1)} reshape(bf16[2,3,32,4,3,64]{5,4,3,2,1,0:T(4,128)(2,1)} %pad_maximum_fusion.1) | data formatting | bytes 589824 | tf_op jit(solution)/shard_map/reshape | solution.py:316
  39.8 0.7 mul.69.wo_ref
  40.5 0.9 convert_reduce_fusion
  41.3 0.6 fusion.34.w_ref
  42.0 0.7 iota_compare_fusion
  42.6 14.1 %shard_map.113.lat_ref = bf16[8,34,64,128]{3,2,1,0:T(8,128)(2,1)} custom-call(bf16[256,128]{1,0:T(8,128)(2,1)} %get-tuple-element.42.sel_ref, bf16[128,4096]{1,0:T(8,128)(2,1)} %copy-done.1, bf16[128,4096]{1,0:T(8,128)(2,1)} %collective-permute-done.peer_ref, bf16[64,64]{1,0:T(8,128)(2,1)} %fusion.34.w_ref), custom_call_target="tpu_custom_call" | custom-call | flops 1073741824 | bytes 8388608 | tf_op jit(solution)/shard_map/pallas_call | solution.py:349
  56.7 1.3 fusion.42
  58.0 5.3 %collective-permute-start.1 = (bf16[1,34,64,128]{3,2,1,0:T(8,128)(2,1)S(1)}, bf16[1,34,64,128]{3,2,1,0:T(8,128)(2,1)}, u32[]{:S(2)}, u32[]{:S(2)}) collective-permute-start(bf16[1,34,64,128]{3,2,1,0:T(8,128)(2,1)S(1)} %get-tuple-element.22), channel_id=1, source_target_pairs={{0,2},{2,4},{4,6},{6,8},{8,10},{10,12},{12,14},{1,3},{3,5},{5,7},{... | collective-permute-start | bytes 1671176 | tf_op jit(solution)/shard_map/ppermute | solution.py:359
  63.3 1.5 collective-permute-start.2
  64.8 18.6 %shard_map.114 = (f32[128,32,128]{2,1,0:T(8,128)}, bf16[128,32,128]{2,1,0:T(8,128)(2,1)}, f32[512,128]{1,0:T(8,128)}) custom-call(bf16[8,34,64,128]{3,2,1,0:T(8,128)(2,1)} %shard_map.113.lat_ref, bf16[192,768]{1,0:T(8,128)(2,1)} %reshape.155.w_ref, bf16[16,128]{1,0:T(8,128)(2,1)} %mul.69.wo_ref), custom_call_target="tpu_custom_call" | custom-call | flops 8589934592 | bytes 8388608 | tf_op jit(solution)/shard_map/pallas_call | solution.py:367
  83.4 1.0 reshape.156
  84.4 2.6 %collective-permute-done.1.low_ref = bf16[1,34,64,128]{3,2,1,0:T(8,128)(2,1)} collective-permute-done((bf16[1,34,64,128]{3,2,1,0:T(8,128)(2,1)S(1)}, bf16[1,34,64,128]{3,2,1,0:T(8,128)(2,1)}, u32[]{:S(2)}, u32[]{:S(2)}) %collective-permute-start.1) | collective-permute-done | bytes 557088 | tf_op jit(solution)/shard_map/ppermute | solution.py:359
  87.0 18.8 %shard_map.115 = (f32[128,32,128]{2,1,0:T(8,128)}, bf16[128,32,128]{2,1,0:T(8,128)(2,1)}, f32[512,128]{1,0:T(8,128)}) custom-call(bf16[8,34,64,128]{3,2,1,0:T(8,128)(2,1)} %shard_map.113.lat_ref, bf16[1,34,64,128]{3,2,1,0:T(8,128)(2,1)} %collective-permute-done.1.low_ref, bf16[1,34,64,128]{3,2,1,0:T(8,128)(2,1)} %collective-permute-done.2.high_ref, ...), custom_call_target="tpu_custom_call" | custom-call | flops 8589934592 | bytes 8388608 | tf_op jit(solution)/shard_map/pallas_call | solution.py:368
  105.8 1.0 reshape.157
  107.2 1.0 convolution_add_fusion
  108.2 16.5 %shard_map.116 = f32[8,16,512]{2,1,0:T(8,128)} custom-call(f32[8,16,512]{2,1,0:T(8,128)} %bitcast.56), custom_call_target="tpu_custom_call" | custom-call | tf_op jit(solution)/shard_map/pallas_call | solution.py:264
  124.7 1.2 fusion.32
  126.0 0.6 reduce_sum.49
  127.5 1.2 fusion.5
  128.9 0.6 multiply_reduce_fusion
  129.5 0.6 fusion.24
  130.3 1.0 fusion.28.in_ref
  131.3 11.4 %shard_map.117 = f32[8,16,512]{2,1,0:T(8,128)} custom-call(f32[8,16,512]{2,1,0:T(8,128)} %fusion.28.in_ref), custom_call_target="tpu_custom_call" | custom-call | tf_op jit(solution)/shard_map/pallas_call | solution.py:264
  142.7 2.1 %fusion.17.r_ref = f32[256,512]{1,0:T(8,128)} fusion(f32[128,512]{1,0:T(8,128)} %bitcast.58, s32[128]{0:T(128)S(1)} %convert_reduce_fusion), kind=kOutput, calls=%fused_computation.35 | convolution fusion | flops 201359360 | bytes 786944 | tf_op jit(solution)/shard_map/ts,sn->tn/dot_general | solution.py:391
  144.8 0.7 broadcast_in_dim.67.wo_ref
  145.6 16.9 %shard_map.118 = (f32[576,128]{1,0:T(8,128)}, f32[4,32,128]{2,1,0:T(8,128)}) custom-call(bf16[8,34,64,128]{3,2,1,0:T(8,128)(2,1)} %shard_map.113.lat_ref, bf16[1,34,64,128]{3,2,1,0:T(8,128)(2,1)} %collective-permute-done.1.low_ref, bf16[1,34,64,128]{3,2,1,0:T(8,128)(2,1)} %collective-permute-done.2.high_ref, f32[128,32,128]{2,1,0:T(8,128)} %get-tuple-element.11.inner_slope, ...), custom_call_target="tpu_custom_call" | custom-call | flops 8589934592 | bytes 8388608 | tf_op jit(solution)/shard_map/pallas_call | solution.py:393
  162.4 1.2 reshape.164
  163.6 0.9 reduce_sum.47
  164.6 1.6 concatenate.31
  166.2 0.7 pad.14
  166.9 18.4 %shard_map.119 = f32[8,56,128]{2,1,0:T(8,128)} custom-call(f32[8,56,128]{2,1,0:T(8,128)} %bitcast.59), custom_call_target="tpu_custom_call" | custom-call | tf_op jit(solution)/shard_map/pallas_call | solution.py:264
  185.4 1.2 slice.93
  186.6 1.3 fusion.44
  187.9 0.9 slice.110
  190.2 1.6 reshape.170
  191.9 1.5 copy.41
  193.6 0.6 slice_multiply_fusion
  194.2 0.9 fusion.4
  (48 shorter events, 2.7 us)
Async XLA Ops:
  0.6 3.4 %copy-start = (bf16[64,128,128]{2,1,0:T(8,128)(2,1)S(1)}, bf16[64,128,128]{2,1,0:T(8,128)(2,1)}, u32[]{:S(2)}) copy-start(bf16[64,128,128]{2,1,0:T(8,128)(2,1)} %param.10) | copy-start | bytes 6291460
  7.4 27.2 %copy-start.5 = (bf16[64,64]{1,0:T(8,128)(2,1)S(1)}, bf16[64,64]{1,0:T(8,128)(2,1)}, u32[]{:S(2)}) copy-start(bf16[64,64]{1,0:T(8,128)(2,1)} %param.15) | copy-start | bytes 24580
  7.4 27.4 %copy-start.2 = (bf16[27,64,32]{1,2,0:T(8,128)(2,1)S(1)}, bf16[27,64,32]{1,2,0:T(8,128)(2,1)}, u32[]{:S(2)}) copy-start(bf16[27,64,32]{1,2,0:T(8,128)(2,1)} %param.16) | copy-start | bytes 331780
  34.5 2.9 %copy-start.1 = (bf16[128,4096]{1,0:T(8,128)(2,1)}, bf16[128,4096]{1,0:T(8,128)(2,1)S(1)}, u32[]{:S(2)}) copy-start(bf16[128,4096]{1,0:T(8,128)(2,1)S(1)} %slice.97.own_ref) | copy-start | bytes 3145732
  34.5 1.2 copy-start.6
  34.5 8.1 %collective-permute-start = (bf16[128,4096]{1,0:T(8,128)(2,1)S(1)}, bf16[128,4096]{1,0:T(8,128)(2,1)}, u32[]{:S(2)}, u32[]{:S(2)}) collective-permute-start(bf16[128,4096]{1,0:T(8,128)(2,1)S(1)} %slice.97.own_ref), channel_id=1, source_target_pairs={{0,1},{1,0},{2,3},{3,2},{4,5},{5,4},{6,7},{7,6},{8,9},{9,8},{10,11... | collective-permute-start | bytes 3145736 | tf_op jit(solution)/shard_map/ppermute | solution.py:198
  58.0 28.9 %collective-permute-start.1 = (bf16[1,34,64,128]{3,2,1,0:T(8,128)(2,1)S(1)}, bf16[1,34,64,128]{3,2,1,0:T(8,128)(2,1)}, u32[]{:S(2)}, u32[]{:S(2)}) collective-permute-start(bf16[1,34,64,128]{3,2,1,0:T(8,128)(2,1)S(1)} %get-tuple-element.22), channel_id=1, source_target_pairs={{0,2},{2,4},{4,6},{6,8},{8,10},{10,12},{12,14},{1,3},{3,5},{5,7},{... | collective-permute-start | bytes 1671176 | tf_op jit(solution)/shard_map/ppermute | solution.py:359
  63.3 23.6 %collective-permute-start.2 = (bf16[1,34,64,128]{3,2,1,0:T(8,128)(2,1)S(1)}, bf16[1,34,64,128]{3,2,1,0:T(8,128)(2,1)}, u32[]{:S(2)}, u32[]{:S(2)}) collective-permute-start(bf16[1,34,64,128]{3,2,1,0:T(8,128)(2,1)S(1)} %get-tuple-element.21), channel_id=1, source_target_pairs={{2,0},{4,2},{6,4},{8,6},{10,8},{12,10},{14,12},{3,1},{5,3},{7,5},{... | collective-permute-start | bytes 1671176 | tf_op jit(solution)/shard_map/ppermute | solution.py:360
  87.0 20.2 %copy-start.4 = (pred[256,128]{1,0:T(32,128)(4,1)S(1)}, pred[256,128]{1,0:T(32,128)(4,1)}, u32[]{:S(2)}) copy-start(pred[256,128]{1,0:T(32,128)(4,1)} %get-tuple-element.40) | copy-start | bytes 98308
  105.8 20.3 %copy-start.8 = (s32[64]{0:T(128)S(1)}, s32[64]{0:T(128)}, u32[]{:S(2)}) copy-start(s32[64]{0:T(128)} %param.13) | copy-start | bytes 772
  125.9 1.4 collective-permute-start.3
  127.4 1.4 copy-start.3
  129.5 15.3 %copy-start.7 = (bf16[4,32]{1,0:T(4,128)(2,1)S(1)}, bf16[4,32]{1,0:T(4,128)(2,1)}, u32[]{:S(2)}) copy-start(bf16[4,32]{1,0:T(4,128)(2,1)} %param.17) | copy-start | bytes 772

commit v4 on v3

--- a/solution.py
+++ b/solution.py
@@ -48,7 +48,7 @@
         out_ref[z, x + 2] = res[:, width:]
         return carry
 
-    lax.fori_loop(0, tiles // 2, body, 0, unroll=4)
+    lax.fori_loop(0, tiles // 2, body, 0, unroll=32)
 
 
 def shifted(array, by):
@@ -100,7 +100,7 @@
                 p_ref[pl.ds(start, rows), :] = heads[d * rows : (d + 1) * rows]
             return carry
 
-        lax.fori_loop(0, GX // 2, body, 0, unroll=2)
+        lax.fori_loop(0, GX // 2, body, 0, unroll=8)
 
 
 def inner_kernel(lat_ref, w_ref, wo_ref, slope_ref, mixed_ref, p_ref):
@@ -167,7 +167,7 @@
             )
             return carry
 
-        lax.fori_loop(0, GX // number, body, 0)
+        lax.fori_loop(0, GX // number, body, 0, unroll=2)
     rows = grad_ref.shape[0]
     step = acc_ref.shape[0] - rows
     grad_ref[...] = acc_ref[:rows, :128] + acc_ref[step:, 128:]

time: 197 us -> 186 us (0.944)
  Pallas kernels: 140 us -> 125 us
  waiting for transfers between devices: 2.6 us -> 7.52 us
    ppermute x1, waiting for transfers between devices: 2.56 us -> 7.48 us  [per_device(): before = lax.ppermute(latent[CZ - 1:], 'slab', up)]
    pallas_call x1, Pallas kernels: 18.8 us -> 13.9 us  [per_device(): call(outer_kernel, shapes, 5, 1 << 33)]
    pallas_call x1, Pallas kernels: 18.6 us -> 13.9 us  [per_device(): inner = call(inner_kernel, shapes, 3, 1 << 33)(latent, w_pair, w_head)]
    pallas_call x1, Pallas kernels: 14.1 us -> 10.4 us  [per_device(): call(lift_kernel, jax.ShapeDtypeStruct((CZ, GX + 2, channels, width), bf1...]
    pallas_call x1, Pallas kernels: 16.9 us -> 14.7 us  [per_device(): call(grad_kernel, (jax.ShapeDtypeStruct((9 * channels, 128), f32), jax.Sh...]
  transfers between devices with their start and end apart: 4 -> 4, of which waited for: 1 -> 1; matrix products, arithmetic and copies ran while one was open for 5% -> 5% of each run, Pallas kernels for 9% -> 7%
where the time goes in v4:
time: 186 us; the launch traced here: 185 us
  Pallas kernels  125 us (67%)
  local copies, waits for them, and re-layouts  20 us (11%)
  other arithmetic  12.3 us (7%)
  matrix products  9.89 us (5%)
  waiting for transfers between devices  7.52 us (4%)
  starting transfers between devices  6.73 us (4%)
  between operations  4.09 us (2%)
    pallas_call x4, Pallas kernels, exchange_call(): pl.pallas_call(functools.partial(kernel, n), out_shape=jax.ShapeDtypeStru...  72.1 us
    pallas_call x1, Pallas kernels, per_device(): call(grad_kernel, (jax.ShapeDtypeStruct((9 * channels, 128), f32), jax.Sh...  14.7 us
    pallas_call x1, Pallas kernels, per_device(): call(outer_kernel, shapes, 5, 1 << 33)  13.9 us
    pallas_call x1, Pallas kernels, per_device(): inner = call(inner_kernel, shapes, 3, 1 << 33)(latent, w_pair, w_head)  13.9 us
    pallas_call x1, Pallas kernels, per_device(): call(lift_kernel, jax.ShapeDtypeStruct((CZ, GX + 2, channels, width), bf1...  10.4 us
    ppermute x1, waiting for transfers between devices, per_device(): before = lax.ppermute(latent[CZ - 1:], 'slab', up)  7.48 us
    ppermute x1, starting transfers between devices, per_device(): before = lax.ppermute(latent[CZ - 1:], 'slab', up)  5.31 us
  transfers between devices with their start and end apart: 4, of which 1 were waited for; matrix products, arithmetic and copies ran while one was open for 5% of the time, Pallas kernels for 7%

profile of v4, /device:TPU:0, one launch (start us, length us, event | category | flops | bytes accessed | tf_op | source)
XLA Modules:
  0.0 185.4 jit_solution(5496873888611055451)
XLA Ops:
  0.6 0.9 fusion.33
  1.6 0.8 select_reduce_fusion.1
  2.5 0.7 multiply_add_fusion.1
  3.3 0.7 iota_compare_fusion.2
  4.0 1.7 convolution_convert_fusion.1
  5.7 0.6 convolution_convert_fusion
  6.3 1.1 pad_maximum_fusion
  7.4 25.8 %shard_map.112 = bf16[8,16,4224]{2,1,0:T(8,128)(2,1)} custom-call(bf16[8,16,4224]{2,1,0:T(8,128)(2,1)} %bitcast.50), custom_call_target="tpu_custom_call" | custom-call | tf_op jit(solution)/shard_map/pallas_call | solution.py:264
  33.2 1.3 slice.97.own_ref
  35.8 1.6 pad_maximum_fusion.1
  37.4 2.4 %reshape.155.w_ref = bf16[192,768]{1,0:T(8,128)(2,1)} reshape(bf16[2,3,32,4,3,64]{5,4,3,2,1,0:T(4,128)(2,1)} %pad_maximum_fusion.1) | data formatting | bytes 589824 | tf_op jit(solution)/shard_map/reshape | solution.py:316
  39.8 0.7 mul.69.wo_ref
  40.5 0.9 convert_reduce_fusion
  41.3 0.6 fusion.34.w_ref
  42.0 0.7 iota_compare_fusion
  42.6 10.4 %shard_map.113.lat_ref = bf16[8,34,64,128]{3,2,1,0:T(8,128)(2,1)} custom-call(bf16[256,128]{1,0:T(8,128)(2,1)} %get-tuple-element.42.sel_ref, bf16[128,4096]{1,0:T(8,128)(2,1)} %copy-done.1, bf16[128,4096]{1,0:T(8,128)(2,1)} %collective-permute-done.peer_ref, bf16[64,64]{1,0:T(8,128)(2,1)} %fusion.34.w_ref), custom_call_target="tpu_custom_call" | custom-call | flops 1073741824 | bytes 8388608 | tf_op jit(solution)/shard_map/pallas_call | solution.py:349
  53.0 1.3 fusion.42
  54.3 5.3 %collective-permute-start.1 = (bf16[1,34,64,128]{3,2,1,0:T(8,128)(2,1)S(1)}, bf16[1,34,64,128]{3,2,1,0:T(8,128)(2,1)}, u32[]{:S(2)}, u32[]{:S(2)}) collective-permute-start(bf16[1,34,64,128]{3,2,1,0:T(8,128)(2,1)S(1)} %get-tuple-element.22), channel_id=1, source_target_pairs={{0,2},{2,4},{4,6},{6,8},{8,10},{10,12},{12,14},{1,3},{3,5},{5,7},{... | collective-permute-start | bytes 1671176 | tf_op jit(solution)/shard_map/ppermute | solution.py:359
  59.6 1.3 collective-permute-start.2
  60.9 13.9 %shard_map.114 = (f32[128,32,128]{2,1,0:T(8,128)}, bf16[128,32,128]{2,1,0:T(8,128)(2,1)}, f32[512,128]{1,0:T(8,128)}) custom-call(bf16[8,34,64,128]{3,2,1,0:T(8,128)(2,1)} %shard_map.113.lat_ref, bf16[192,768]{1,0:T(8,128)(2,1)} %reshape.155.w_ref, bf16[16,128]{1,0:T(8,128)(2,1)} %mul.69.wo_ref), custom_call_target="tpu_custom_call" | custom-call | flops 8589934592 | bytes 8388608 | tf_op jit(solution)/shard_map/pallas_call | solution.py:367
  74.8 1.0 reshape.156
  75.8 7.5 %collective-permute-done.1.low_ref = bf16[1,34,64,128]{3,2,1,0:T(8,128)(2,1)} collective-permute-done((bf16[1,34,64,128]{3,2,1,0:T(8,128)(2,1)S(1)}, bf16[1,34,64,128]{3,2,1,0:T(8,128)(2,1)}, u32[]{:S(2)}, u32[]{:S(2)}) %collective-permute-start.1) | collective-permute-done | bytes 557088 | tf_op jit(solution)/shard_map/ppermute | solution.py:359
  83.2 13.9 %shard_map.115 = (f32[128,32,128]{2,1,0:T(8,128)}, bf16[128,32,128]{2,1,0:T(8,128)(2,1)}, f32[512,128]{1,0:T(8,128)}) custom-call(bf16[8,34,64,128]{3,2,1,0:T(8,128)(2,1)} %shard_map.113.lat_ref, bf16[1,34,64,128]{3,2,1,0:T(8,128)(2,1)} %collective-permute-done.1.low_ref, bf16[1,34,64,128]{3,2,1,0:T(8,128)(2,1)} %collective-permute-done.2.high_ref, ...), custom_call_target="tpu_custom_call" | custom-call | flops 8589934592 | bytes 8388608 | tf_op jit(solution)/shard_map/pallas_call | solution.py:368
  97.1 1.0 reshape.157
  98.6 1.0 convolution_add_fusion
  99.6 16.5 %shard_map.116 = f32[8,16,512]{2,1,0:T(8,128)} custom-call(f32[8,16,512]{2,1,0:T(8,128)} %bitcast.56), custom_call_target="tpu_custom_call" | custom-call | tf_op jit(solution)/shard_map/pallas_call | solution.py:264
  116.1 1.2 fusion.32
  117.4 0.6 reduce_sum.49
  118.9 1.2 fusion.5
  120.2 0.6 multiply_reduce_fusion
  120.9 0.6 fusion.24
  121.6 1.0 fusion.28.in_ref
  122.6 11.4 %shard_map.117 = f32[8,16,512]{2,1,0:T(8,128)} custom-call(f32[8,16,512]{2,1,0:T(8,128)} %fusion.28.in_ref), custom_call_target="tpu_custom_call" | custom-call | tf_op jit(solution)/shard_map/pallas_call | solution.py:264
  134.1 2.1 %fusion.17.r_ref = f32[256,512]{1,0:T(8,128)} fusion(f32[128,512]{1,0:T(8,128)} %bitcast.58, s32[128]{0:T(128)S(1)} %convert_reduce_fusion), kind=kOutput, calls=%fused_computation.35 | convolution fusion | flops 201359360 | bytes 786944 | tf_op jit(solution)/shard_map/ts,sn->tn/dot_general | solution.py:391
  136.2 0.7 broadcast_in_dim.67.wo_ref
  136.9 14.7 %shard_map.118 = (f32[576,128]{1,0:T(8,128)}, f32[4,32,128]{2,1,0:T(8,128)}) custom-call(bf16[8,34,64,128]{3,2,1,0:T(8,128)(2,1)} %shard_map.113.lat_ref, bf16[1,34,64,128]{3,2,1,0:T(8,128)(2,1)} %collective-permute-done.1.low_ref, bf16[1,34,64,128]{3,2,1,0:T(8,128)(2,1)} %collective-permute-done.2.high_ref, f32[128,32,128]{2,1,0:T(8,128)} %get-tuple-element.11.inner_slope, ...), custom_call_target="tpu_custom_call" | custom-call | flops 8589934592 | bytes 8388608 | tf_op jit(solution)/shard_map/pallas_call | solution.py:393
  151.6 1.2 reshape.164
  152.8 0.9 reduce_sum.47
  153.8 1.6 concatenate.31
  155.4 0.7 pad.14
  156.1 18.4 %shard_map.119 = f32[8,56,128]{2,1,0:T(8,128)} custom-call(f32[8,56,128]{2,1,0:T(8,128)} %bitcast.59), custom_call_target="tpu_custom_call" | custom-call | tf_op jit(solution)/shard_map/pallas_call | solution.py:264
  174.5 1.2 slice.93
  175.7 1.3 fusion.44
  177.1 0.9 slice.110
  179.3 1.6 reshape.170
  181.0 1.5 copy.41
  182.8 0.6 slice_multiply_fusion
  183.3 0.9 fusion.4
  (48 shorter events, 2.7 us)
Async XLA Ops:
  0.6 3.4 %copy-start = (bf16[64,128,128]{2,1,0:T(8,128)(2,1)S(1)}, bf16[64,128,128]{2,1,0:T(8,128)(2,1)}, u32[]{:S(2)}) copy-start(bf16[64,128,128]{2,1,0:T(8,128)(2,1)} %param.10) | copy-start | bytes 6291460
  7.4 27.2 %copy-start.5 = (bf16[64,64]{1,0:T(8,128)(2,1)S(1)}, bf16[64,64]{1,0:T(8,128)(2,1)}, u32[]{:S(2)}) copy-start(bf16[64,64]{1,0:T(8,128)(2,1)} %param.15) | copy-start | bytes 24580
  7.4 27.4 %copy-start.2 = (bf16[27,64,32]{1,2,0:T(8,128)(2,1)S(1)}, bf16[27,64,32]{1,2,0:T(8,128)(2,1)}, u32[]{:S(2)}) copy-start(bf16[27,64,32]{1,2,0:T(8,128)(2,1)} %param.16) | copy-start | bytes 331780
  34.5 2.9 %copy-start.1 = (bf16[128,4096]{1,0:T(8,128)(2,1)}, bf16[128,4096]{1,0:T(8,128)(2,1)S(1)}, u32[]{:S(2)}) copy-start(bf16[128,4096]{1,0:T(8,128)(2,1)S(1)} %slice.97.own_ref) | copy-start | bytes 3145732
  34.5 1.2 copy-start.6
  34.5 8.1 %collective-permute-start = (bf16[128,4096]{1,0:T(8,128)(2,1)S(1)}, bf16[128,4096]{1,0:T(8,128)(2,1)}, u32[]{:S(2)}, u32[]{:S(2)}) collective-permute-start(bf16[128,4096]{1,0:T(8,128)(2,1)S(1)} %slice.97.own_ref), channel_id=1, source_target_pairs={{0,1},{1,0},{2,3},{3,2},{4,5},{5,4},{6,7},{7,6},{8,9},{9,8},{10,11... | collective-permute-start | bytes 3145736 | tf_op jit(solution)/shard_map/ppermute | solution.py:198
  54.3 28.9 %collective-permute-start.1 = (bf16[1,34,64,128]{3,2,1,0:T(8,128)(2,1)S(1)}, bf16[1,34,64,128]{3,2,1,0:T(8,128)(2,1)}, u32[]{:S(2)}, u32[]{:S(2)}) collective-permute-start(bf16[1,34,64,128]{3,2,1,0:T(8,128)(2,1)S(1)} %get-tuple-element.22), channel_id=1, source_target_pairs={{0,2},{2,4},{4,6},{6,8},{8,10},{10,12},{12,14},{1,3},{3,5},{5,7},{... | collective-permute-start | bytes 1671176 | tf_op jit(solution)/shard_map/ppermute | solution.py:359
  59.6 23.6 %collective-permute-start.2 = (bf16[1,34,64,128]{3,2,1,0:T(8,128)(2,1)S(1)}, bf16[1,34,64,128]{3,2,1,0:T(8,128)(2,1)}, u32[]{:S(2)}, u32[]{:S(2)}) collective-permute-start(bf16[1,34,64,128]{3,2,1,0:T(8,128)(2,1)S(1)} %get-tuple-element.21), channel_id=1, source_target_pairs={{2,0},{4,2},{6,4},{8,6},{10,8},{12,10},{14,12},{3,1},{5,3},{7,5},{... | collective-permute-start | bytes 1671176 | tf_op jit(solution)/shard_map/ppermute | solution.py:360
  83.2 15.3 %copy-start.4 = (pred[256,128]{1,0:T(32,128)(4,1)S(1)}, pred[256,128]{1,0:T(32,128)(4,1)}, u32[]{:S(2)}) copy-start(pred[256,128]{1,0:T(32,128)(4,1)} %get-tuple-element.40) | copy-start | bytes 98308
  97.1 20.3 %copy-start.8 = (s32[64]{0:T(128)S(1)}, s32[64]{0:T(128)}, u32[]{:S(2)}) copy-start(s32[64]{0:T(128)} %param.13) | copy-start | bytes 772
  117.3 1.4 collective-permute-start.3
  118.8 1.4 copy-start.3
  120.9 15.3 %copy-start.7 = (bf16[4,32]{1,0:T(4,128)(2,1)S(1)}, bf16[4,32]{1,0:T(4,128)(2,1)}, u32[]{:S(2)}) copy-start(bf16[4,32]{1,0:T(4,128)(2,1)} %param.17) | copy-start | bytes 772
